TPU v7x, 32 devices: a whole 2x2x4 slice. The times are simulated.
32 devices in a mesh: dp: 8 (over y, x, core), tensor: 4 (over z).
Axes of the slice: x: 2, y: 2, z: 4, core: 2. Of those that a mesh axis runs over, the one named last changes fastest.
Arguments:
- inputs: bfloat16 [512, 24, 768], P('tensor', 'dp'), may hold values from -6 to 6
- cotangent: bfloat16 [512, 24, 768], P('tensor', 'dp'), may hold values from -6 to 6
- norm_gain: bfloat16 [2, 2, 768], P(None, None, ('dp', 'tensor')), may hold values from 0.25 to 1.75
- norm_shift: bfloat16 [2, 2, 768], P(None, None, ('dp', 'tensor')), may hold values from -3 to 3
- attention_weight: bfloat16 [2, 3, 768, 768], P(None, None, 'dp', 'tensor'), may hold values from -0.21875 to 0.21875
- attention_bias: bfloat16 [2, 2, 768], P(None, None, ('dp', 'tensor')), may hold values from -3 to 3
- output_weight: bfloat16 [2, 768, 768], P(None, 'tensor', 'dp'), may hold values from -0.875 to 0.875
- output_bias: bfloat16 [2, 768], P(None, ('dp', 'tensor')), may hold values from -3 to 3
- expand_weight: bfloat16 [2, 768, 3072], P(None, 'dp', 'tensor'), may hold values from -0.21875 to 0.21875
- expand_bias: bfloat16 [2, 3072], P(None, ('dp', 'tensor')), may hold values from -3 to 3
- contract_weight: bfloat16 [2, 3072, 768], P(None, 'tensor', 'dp'), may hold values from -0.15625 to 0.15625
- contract_bias: bfloat16 [2, 768], P(None, ('dp', 'tensor')), may hold values from -3 to 3
Outputs:
- outputs: bfloat16 [512, 24, 768], P('tensor', 'dp')
- first_input_gradient: float32 [512, 24, 768], P('tensor', 'dp')
- gain_gradient: float32 [2, 2, 768], P(None, None, ('dp', 'tensor'))
- shift_gradient: float32 [2, 2, 768], P(None, None, ('dp', 'tensor'))
- attention_gradient: float32 [2, 3, 768, 768], P(None, None, 'dp', 'tensor')
- attention_bias_gradient: float32 [2, 2, 768], P(None, None, ('dp', 'tensor'))
- output_gradient: float32 [2, 768, 768], P(None, 'tensor', 'dp')
- output_bias_gradient: float32 [2, 768], P(None, ('dp', 'tensor'))
- expand_gradient: float32 [2, 768, 3072], P(None, 'dp', 'tensor')
- expand_bias_gradient: float32 [2, 3072], P(None, ('dp', 'tensor'))
- contract_gradient: float32 [2, 3072, 768], P(None, 'tensor', 'dp')
- contract_bias_grads: float32 [2, 768], P(None, ('dp', 'tensor'))
All inputs are finite; a program needn't handle non-finite values.
Results may differ from a plain program's by a relative error of at most 0.019.
Values may be sent and summed in bfloat16 or wider, within the bound.
A program may use at most 192 MiB of HBM per device.

v0:
```python
import jax
import jax.numpy as jnp
from jax import lax
from jax.sharding import PartitionSpec as P

D = 768
HEAD = 64
FF = 3072


EPSILON = 1e-05


def norm_stats(rows):
    average = jnp.mean(rows, axis=-1, keepdims=True)
    centred = rows - average
    inverse = lax.rsqrt(jnp.mean(centred * centred, axis=-1, keepdims=True) + EPSILON)
    return (centred * inverse, inverse)


def norm_back(incoming, gain, scaled, inverse):
    weighted = incoming * gain
    first = jnp.mean(weighted, axis=-1, keepdims=True)
    second = jnp.mean(weighted * scaled, axis=-1, keepdims=True)
    return inverse * (weighted - first - scaled * second)


def smooth_unit(values):
    return jax.nn.gelu(values, approximate=True)


def row_products(pattern, source, matrix):
    return jnp.einsum(pattern, source, matrix, preferred_element_type=jnp.float32)


def split_heads(rows):
    length, sequences, columns = rows.shape
    return (
        rows.reshape(length, sequences, columns // HEAD, HEAD)
        .transpose(1, 2, 0, 3)
        .reshape(-1, length, HEAD)
    )


def merge_heads(items, sequences):
    count, length, width = items.shape
    return (
        items.reshape(sequences, count // sequences, length, width)
        .transpose(2, 0, 1, 3)
        .reshape(length, sequences, -1)
    )


def causal_mask(length):
    later = lax.broadcasted_iota(jnp.int32, (length, length), 0)
    earlier = lax.broadcasted_iota(jnp.int32, (length, length), 1)
    return later >= earlier


def attend_forward(triple):
    query, keys, values = triple
    scale = query.shape[-1] ** (-0.5)
    scores = jnp.einsum("qd,kd->qk", query, keys, preferred_element_type=jnp.float32) * scale
    scores = jnp.where(causal_mask(query.shape[0]), scores, -1e30)
    largest = jnp.max(scores, axis=-1, keepdims=True)
    powers = jnp.exp(scores - largest)
    totals = jnp.sum(powers, axis=-1, keepdims=True)
    probs = (powers / totals).astype(jnp.bfloat16)
    context = jnp.dot(probs, values, preferred_element_type=jnp.float32)
    return (context.astype(jnp.bfloat16), (largest + jnp.log(totals))[:, 0])


def attend_backward(items):
    query, keys, values, logsum, grad_context = items
    scale = query.shape[-1] ** (-0.5)
    scores = jnp.einsum("qd,kd->qk", query, keys, preferred_element_type=jnp.float32) * scale
    scores = jnp.where(causal_mask(query.shape[0]), scores, -1e30)
    probs = jnp.exp(scores - logsum[:, None])
    grad_probs = jnp.einsum("qd,kd->qk", grad_context, values, preferred_element_type=jnp.float32)
    inner = jnp.sum(grad_probs * probs, axis=-1, keepdims=True)
    grad_scores = (probs * (grad_probs - inner)).astype(jnp.bfloat16)
    grad_query = jnp.dot(grad_scores, keys, preferred_element_type=jnp.float32) * scale
    grad_keys = (
        jnp.einsum("qk,qd->kd", grad_scores, query, preferred_element_type=jnp.float32) * scale
    )
    grad_values = jnp.einsum(
        "qk,qd->kd", probs.astype(jnp.bfloat16), grad_context, preferred_element_type=jnp.float32
    )
    return (grad_query, grad_keys, grad_values)


def gather_weights(attention_weight, output_weight, expand_weight, contract_weight, layer):
    return (
        lax.all_gather(attention_weight[layer], "dp", axis=1, tiled=True),
        lax.all_gather(output_weight[layer], "dp", axis=1, tiled=True),
        lax.all_gather(expand_weight[layer], "dp", axis=0, tiled=True),
        lax.all_gather(contract_weight[layer], "dp", axis=1, tiled=True),
    )


def on_device(
    inputs,
    cotangent,
    norm_gain,
    norm_shift,
    attention_weight,
    attention_bias,
    output_weight,
    output_bias,
    expand_weight,
    expand_bias,
    contract_weight,
    contract_bias,
):
    shared = (
        lax.all_gather(norm_gain, ("dp", "tensor"), axis=2, tiled=True),
        lax.all_gather(norm_shift, ("dp", "tensor"), axis=2, tiled=True),
        lax.all_gather(attention_bias, ("dp", "tensor"), axis=2, tiled=True),
        lax.all_gather(output_bias, ("dp", "tensor"), axis=1, tiled=True),
        lax.all_gather(expand_bias, ("dp", "tensor"), axis=1, tiled=True),
        lax.all_gather(contract_bias, ("dp", "tensor"), axis=1, tiled=True),
    )
    gains, shifts, attention_shift, output_shift, expand_shift, contract_shift = [
        item.astype(jnp.float32) for item in shared
    ]
    layers = attention_weight.shape[0]
    head_width = attention_weight.shape[3]
    hidden_width = expand_weight.shape[2]
    head_start = lax.axis_index("tensor") * head_width
    hidden_start = lax.axis_index("tensor") * hidden_width
    sequences = inputs.shape[1]
    residual = inputs.astype(jnp.float32)
    stored = []
    for layer in range(layers):
        layer_parameters = gather_weights(
            attention_weight, output_weight, expand_weight, contract_weight, layer
        )
        scaled, inverse = norm_stats(residual)
        normed = (scaled * gains[layer, 0] + shifts[layer, 0]).astype(jnp.bfloat16)
        normed_all = lax.all_gather(normed, "tensor", axis=0, tiled=True)
        projected = jnp.einsum(
            "lsd,cde->lsce", normed_all, layer_parameters[0], preferred_element_type=jnp.float32
        )
        query_shift = lax.dynamic_slice_in_dim(attention_shift[layer, 0], head_start, head_width, 0)
        value_shift = lax.dynamic_slice_in_dim(attention_shift[layer, 1], head_start, head_width, 0)
        query = (projected[:, :, 0] + query_shift).astype(jnp.bfloat16)
        keys = projected[:, :, 1].astype(jnp.bfloat16)
        values = (projected[:, :, 2] + value_shift).astype(jnp.bfloat16)
        context_items, logsum = lax.map(
            attend_forward, (split_heads(query), split_heads(keys), split_heads(values))
        )
        context = merge_heads(context_items, sequences)
        attended = lax.psum_scatter(
            row_products("lse,ed->lsd", context, layer_parameters[1]).astype(jnp.bfloat16),
            "tensor",
            scatter_dimension=0,
            tiled=True,
        ).astype(jnp.float32)
        middle = residual + attended + output_shift[layer]
        scaled, inverse = norm_stats(middle)
        expanded = (scaled * gains[layer, 1] + shifts[layer, 1]).astype(jnp.bfloat16)
        expanded_gathered_rows = lax.all_gather(expanded, "tensor", axis=0, tiled=True)
        hidden_shift = lax.dynamic_slice_in_dim(expand_shift[layer], hidden_start, hidden_width, 0)
        hidden = (
            jnp.einsum(
                "ybz,zu->ybu",
                expanded_gathered_rows,
                layer_parameters[2],
                preferred_element_type=jnp.float32,
            )
            + hidden_shift
        )
        active_rows = smooth_unit(hidden).astype(jnp.bfloat16)
        shrunk = lax.psum_scatter(
            row_products("wpx,xy->wpy", active_rows, layer_parameters[3]).astype(jnp.bfloat16),
            "tensor",
            scatter_dimension=0,
            tiled=True,
        ).astype(jnp.float32)
        kept = None
        stored.append(
            (
                residual,
                normed_all,
                query,
                keys,
                values,
                logsum,
                context,
                middle,
                expanded_gathered_rows,
                hidden,
                active_rows,
                kept,
            )
        )
        residual = middle + shrunk + contract_shift[layer]
    outputs = residual.astype(jnp.bfloat16)
    upstream = cotangent.astype(jnp.float32)
    weight_parts = []
    gain_parts = []
    shift_parts = []
    attention_parts = []
    output_parts = []
    expand_parts = []
    contract_parts = []
    for layer in reversed(range(layers)):
        (
            before,
            normed_all,
            query,
            keys,
            values,
            logsum,
            context,
            middle,
            expanded_gathered_rows,
            hidden,
            active_rows,
            kept,
        ) = stored[layer]
        layer_parameters = gather_weights(
            attention_weight, output_weight, expand_weight, contract_weight, layer
        )
        contract_shift_grad = jnp.sum(upstream, axis=(0, 1))
        upstream_gathered = lax.all_gather(
            upstream.astype(jnp.bfloat16), "tensor", axis=0, tiled=True
        )
        contract_grad = jnp.einsum(
            "gmc,gmk->ck", active_rows, upstream_gathered, preferred_element_type=jnp.float32
        )
        grad_active = jnp.einsum(
            "xni,ki->xnk",
            upstream_gathered,
            layer_parameters[3],
            preferred_element_type=jnp.float32,
        )
        unused, pull_unit = jax.vjp(smooth_unit, hidden)
        grad_hidden = pull_unit(grad_active)[0]
        expand_shift_local = jnp.sum(grad_hidden, axis=(0, 1))
        hidden_gradient_reduced = grad_hidden.astype(jnp.bfloat16)
        expand_grad = jnp.einsum(
            "aye,ayp->ep",
            expanded_gathered_rows,
            hidden_gradient_reduced,
            preferred_element_type=jnp.float32,
        )
        grad_second = lax.psum_scatter(
            row_products("xgj,oj->xgo", hidden_gradient_reduced, layer_parameters[2]).astype(
                jnp.bfloat16
            ),
            "tensor",
            scatter_dimension=0,
            tiled=True,
        ).astype(jnp.float32)
        scaled, inverse = norm_stats(middle)
        second_gain = jnp.sum(grad_second * scaled, axis=(0, 1))
        second_shift = jnp.sum(grad_second, axis=(0, 1))
        grad_middle = upstream + norm_back(grad_second, gains[layer, 1], scaled, inverse)
        output_shift_grad = jnp.sum(grad_middle, axis=(0, 1))
        middle_all = lax.all_gather(grad_middle.astype(jnp.bfloat16), "tensor", axis=0, tiled=True)
        output_grad = jnp.einsum(
            "lse,lsd->ed", context, middle_all, preferred_element_type=jnp.float32
        )
        grad_context = jnp.einsum(
            "lsd,ed->lse", middle_all, layer_parameters[1], preferred_element_type=jnp.float32
        ).astype(jnp.bfloat16)
        grad_query, grad_keys, grad_values = lax.map(
            attend_backward,
            (
                split_heads(query),
                split_heads(keys),
                split_heads(values),
                logsum,
                split_heads(grad_context),
            ),
        )
        grad_query = merge_heads(grad_query, sequences)
        grad_keys = merge_heads(grad_keys, sequences)
        grad_values = merge_heads(grad_values, sequences)
        attention_shift_local = jnp.stack(
            [jnp.sum(grad_query, axis=(0, 1)), jnp.sum(grad_values, axis=(0, 1))]
        )
        grad_projected = jnp.stack([grad_query, grad_keys, grad_values], axis=2).astype(
            jnp.bfloat16
        )
        attention_grad = jnp.einsum(
            "lsd,lsce->cde", normed_all, grad_projected, preferred_element_type=jnp.float32
        )
        grad_first = lax.psum_scatter(
            row_products("lsce,cde->lsd", grad_projected, layer_parameters[0]).astype(jnp.bfloat16),
            "tensor",
            scatter_dimension=0,
            tiled=True,
        ).astype(jnp.float32)
        scaled, inverse = norm_stats(before)
        first_gain = jnp.sum(grad_first * scaled, axis=(0, 1))
        first_shift = jnp.sum(grad_first, axis=(0, 1))
        upstream = grad_middle + norm_back(grad_first, gains[layer, 0], scaled, inverse)
        weight_parts.insert(
            0,
            (
                lax.psum_scatter(attention_grad, "dp", scatter_dimension=1, tiled=True),
                lax.psum_scatter(output_grad, "dp", scatter_dimension=1, tiled=True),
                lax.psum_scatter(expand_grad, "dp", scatter_dimension=0, tiled=True),
                lax.psum_scatter(contract_grad, "dp", scatter_dimension=1, tiled=True),
            ),
        )
        gain_parts.insert(0, jnp.stack([first_gain, second_gain]))
        shift_parts.insert(0, jnp.stack([first_shift, second_shift]))
        attention_parts.insert(
            0,
            lax.dynamic_update_slice(
                jnp.zeros((2, D), jnp.float32), attention_shift_local, (jnp.int32(0), head_start)
            ),
        )
        output_parts.insert(0, output_shift_grad)
        expand_parts.insert(
            0,
            lax.dynamic_update_slice(
                jnp.zeros((FF,), jnp.float32), expand_shift_local, (hidden_start,)
            ),
        )
        contract_parts.insert(0, contract_shift_grad)
    small = (
        lax.psum_scatter(jnp.stack(gain_parts), ("dp", "tensor"), scatter_dimension=2, tiled=True),
        lax.psum_scatter(jnp.stack(shift_parts), ("dp", "tensor"), scatter_dimension=2, tiled=True),
        lax.psum_scatter(
            jnp.stack(attention_parts), ("dp", "tensor"), scatter_dimension=2, tiled=True
        ),
        lax.psum_scatter(
            jnp.stack(output_parts), ("dp", "tensor"), scatter_dimension=1, tiled=True
        ),
        lax.psum_scatter(
            jnp.stack(expand_parts), ("dp", "tensor"), scatter_dimension=1, tiled=True
        ),
        lax.psum_scatter(
            jnp.stack(contract_parts), ("dp", "tensor"), scatter_dimension=1, tiled=True
        ),
    )
    attention_out = jnp.stack([part[0] for part in weight_parts])
    output_out = jnp.stack([part[1] for part in weight_parts])
    expand_out = jnp.stack([part[2] for part in weight_parts])
    contract_out = jnp.stack([part[3] for part in weight_parts])
    return (
        outputs,
        upstream,
        small[0],
        small[1],
        attention_out,
        small[2],
        output_out,
        small[3],
        expand_out,
        small[4],
        contract_out,
        small[5],
    )


def solution(mesh):
    return jax.shard_map(
        on_device,
        mesh=mesh,
        in_specs=(
            P("tensor", "dp", None),
            P("tensor", "dp", None),
            P(None, None, ("dp", "tensor")),
            P(None, None, ("dp", "tensor")),
            P(None, None, "dp", "tensor"),
            P(None, None, ("dp", "tensor")),
            P(None, "tensor", "dp"),
            P(None, ("dp", "tensor")),
            P(None, "dp", "tensor"),
            P(None, ("dp", "tensor")),
            P(None, "tensor", "dp"),
            P(None, ("dp", "tensor")),
        ),
        out_specs=(
            P("tensor", "dp", None),
            P("tensor", "dp", None),
            P(None, None, ("dp", "tensor")),
            P(None, None, ("dp", "tensor")),
            P(None, None, "dp", "tensor"),
            P(None, None, ("dp", "tensor")),
            P(None, "tensor", "dp"),
            P(None, ("dp", "tensor")),
            P(None, "dp", "tensor"),
            P(None, ("dp", "tensor")),
            P(None, "tensor", "dp"),
            P(None, ("dp", "tensor")),
        ),
        check_vma=False,
    )
```

profile of v0, /device:TPU:0, one launch (start us, length us, event | category | flops | bytes accessed | tf_op | source)
XLA Modules:
  0.0 1839.4 jit_solution(5161772841292436414)
XLA Ops:
  10.9 72.8 %all_gather.75 = bf16[2,2,768]{1,0,2:T(2,128)(2,1)S(1)} all-gather(bf16[2,2,24]{1,0,2:T(2,128)(2,1)S(1)} %copy.124), channel_id=1, replica_groups=mesh['dp'=8,'tensor'=4] {'dp','tensor'}, dimensions={2}, use_global_device_ids=true | all-gather | bytes 6336 | tf_op jit(solution)/shard_map/all_gather | solution.py:117
  83.8 66.7 %all_gather.74 = bf16[2,2,768]{1,0,2:T(2,128)(2,1)S(1)} all-gather(bf16[2,2,24]{1,0,2:T(2,128)(2,1)S(1)} %copy.123), channel_id=1, replica_groups=mesh['dp'=8,'tensor'=4] {'dp','tensor'}, dimensions={2}, use_global_device_ids=true | all-gather | bytes 6336 | tf_op jit(solution)/shard_map/all_gather | solution.py:116
  150.7 9.7 slice_reduce_fusion.1
  160.7 9.9 slice_reduce_fusion
  173.6 9.3 all-gather.1
  184.6 72.1 %all_gather.78 = bf16[2,2,768]{1,0,2:T(2,128)(2,1)S(1)} all-gather(bf16[2,2,24]{1,0,2:T(2,128)(2,1)S(1)} %copy.127), channel_id=1, replica_groups=mesh['dp'=8,'tensor'=4] {'dp','tensor'}, dimensions={2}, use_global_device_ids=true | all-gather | bytes 6336 | tf_op jit(solution)/shard_map/all_gather | solution.py:118
  260.0 12.4 all-gather
  274.3 3.2 fusion.100
  281.7 28.0 %while.52 = (s32[]{:T(128)}, bf16[9,512,64]{1,2,0:T(8,128)(2,1)S(1)}, f32[9,512]{1,0:T(8,128)}, bf16[9,512,64]{2,1,0:T(8,128)(2,1)S(1)}, bf16[9,512,64]{2,1,0:T(...) while((s32[]{:T(128)}, bf16[9,512,64]{1,2,0:T(8,128)(2,1)S(1)}, f32[9,512]{1,0:T(8,128)}, ...), condition=%wide.region_5.6_spmd, body=%wide.region_2.5_spmd.sunk | while | flops 69500416 | bytes 3627105 | solution.py:149
  309.7 3.4 convolution_convert_fusion.7
  314.9 65.8 %all-gather.8 = bf16[32,24,2]{1,2,0:T(2,128)(2,1)S(1)} all-gather(bf16[1,24,2]{1,2,0:T(2,128)(2,1)S(1)} %bitcast.497), channel_id=1, replica_groups=mesh['dp'=8,'tensor'=4] {'dp','tensor'}, dimensions={0}, use_global_device_ids=true | all-gather | bytes 3168 | tf_op jit(solution)/shard_map/all_gather | solution.py:119
  385.5 64.5 %all-gather.9 = bf16[32,96,2]{1,2,0:T(2,128)(2,1)S(1)} all-gather(bf16[1,96,2]{1,2,0:T(2,128)(2,1)S(1)} %bitcast.498), channel_id=1, replica_groups=mesh['dp'=8,'tensor'=4] {'dp','tensor'}, dimensions={0}, use_global_device_ids=true | all-gather | bytes 12672 | tf_op jit(solution)/shard_map/all_gather | solution.py:120
  450.8 6.1 fusion.155
  457.4 7.2 convolution_convert_fusion.6
  465.3 68.6 %all-gather.10 = bf16[32,24,2]{1,2,0:T(2,128)(2,1)S(1)} all-gather(bf16[1,24,2]{1,2,0:T(2,128)(2,1)S(1)} %bitcast.499), channel_id=1, replica_groups=mesh['dp'=8,'tensor'=4] {'dp','tensor'}, dimensions={0}, use_global_device_ids=true | all-gather | bytes 3168 | tf_op jit(solution)/shard_map/all_gather | solution.py:121
  538.3 10.5 all-gather.5
  553.1 14.1 all-gather.4
  567.2 2.6 copy.140
  569.9 16.1 all-gather.28.cloned.1.call-done
  585.9 3.2 fusion.96
  602.2 34.2 %while.53 = (s32[]{:T(128)}, bf16[9,512,64]{1,2,0:T(8,128)(2,1)}, f32[9,512]{1,0:T(8,128)}, bf16[9,512,64]{2,1,0:T(8,128)(2,1)}, bf16[9,512,64]{2,1,0:T(8,128)(2...) while((s32[]{:T(128)}, bf16[9,512,64]{1,2,0:T(8,128)(2,1)}, f32[9,512]{1,0:T(8,128)}, ...), condition=%wide.region_15.16_spmd, body=%wide.region_12.15_spmd.sunk | while | flops 69500416 | bytes 3627105 | solution.py:149
  636.5 3.8 convolution_convert_fusion.5
  641.1 46.2 %reduce-scatter.37.cloned.1.call-done = bf16[128,3,768]{2,0,1:T(8,128)(2,1)} async-done(((bf16[512,3,768]{2,0,1:T(8,128)(2,1)}), bf16[128,3,768]{2,0,1:T(8,128)(2,1)}) %reduce-scatter.37.cloned.1.call-update) | async-done | bytes 589840 | tf_op jit(solution)/shard_map/reduce_scatter | solution.py:153
  693.4 46.9 %all-gather.30.cloned.1.call-done = bf16[512,3,768]{2,0,1:T(8,128)(2,1)} async-done(((bf16[128,3,768]{2,0,1:T(8,128)(2,1)}), bf16[512,3,768]{2,0,1:T(8,128)(2,1)}) %all-gather.30.cloned.1.call-update) | async-done | bytes 2359312 | tf_op jit(solution)/shard_map/all_gather | solution.py:162
  740.3 6.2 fusion.152
  746.4 18.2 all-gather.46.cloned.1.call-done
  764.6 51.5 %all-gather.32.cloned.1.call-done = bf16[512,3,768]{2,0,1:T(8,128)(2,1)} async-done(((bf16[128,3,768]{2,0,1:T(8,128)(2,1)}), bf16[512,3,768]{2,0,1:T(8,128)(2,1)}) %all-gather.32.cloned.1.call-update) | async-done | bytes 2359312 | tf_op jit(solution)/shard_map/all_gather | solution.py:226
  816.0 8.7 fusion.196
  826.2 3.4 convolution_convert_fusion.3
  829.7 7.2 convolution_convert_fusion.4
  837.4 39.1 %reduce-scatter.41.cloned.1.call-done = bf16[128,3,768]{2,0,1:T(8,128)(2,1)} async-done(((bf16[512,3,768]{2,0,1:T(8,128)(2,1)}), bf16[128,3,768]{2,0,1:T(8,128)(2,1)}) %reduce-scatter.41.cloned.1.call-update) | async-done | bytes 589840 | tf_op jit(solution)/shard_map/reduce_scatter | solution.py:248
  879.9 46.3 %reduce-scatter.39.cloned.1.call-done = bf16[128,3,768]{2,0,1:T(8,128)(2,1)} async-done(((bf16[512,3,768]{2,0,1:T(8,128)(2,1)}), bf16[128,3,768]{2,0,1:T(8,128)(2,1)}) %reduce-scatter.39.cloned.1.call-update) | async-done | bytes 589840 | tf_op jit(solution)/shard_map/reduce_scatter | solution.py:174
  926.3 3.5 fusion.182
  933.5 47.8 %all-gather.34.cloned.1.call-done = bf16[512,3,768]{2,0,1:T(8,128)(2,1)} async-done(((bf16[128,3,768]{2,0,1:T(8,128)(2,1)}), bf16[512,3,768]{2,0,1:T(8,128)(2,1)}) %all-gather.34.cloned.1.call-update) | async-done | bytes 2359312 | tf_op jit(solution)/shard_map/all_gather | solution.py:261
  986.6 75.6 %while.54 = (s32[]{:T(128)}, f32[9,512,64]{1,2,0:T(8,128)}, bf16[9,512,64]{1,2,0:T(8,128)(2,1)}, f32[9,512,64]{1,2,0:T(8,128)S(1)}, bf16[9,512,64]{2,1,0:T(8,128...) while((s32[]{:T(128)}, f32[9,512,64]{1,2,0:T(8,128)}, ...), condition=%wide.region_25.26_spmd, body=%wide.region_23.25_spmd.sunk | while | flops 170458624 | bytes 9190513 | solution.py:268
  1065.7 3.5 bitcast_convert_fusion.1
  1069.2 46.8 %reduce-scatter.43.cloned.1.call-done = bf16[128,3,768]{2,0,1:T(8,128)(2,1)} async-done(((bf16[512,3,768]{2,0,1:T(8,128)(2,1)}), bf16[128,3,768]{2,0,1:T(8,128)(2,1)}) %reduce-scatter.43.cloned.1.call-update) | async-done | bytes 589840 | tf_op jit(solution)/shard_map/reduce_scatter | solution.py:290
  1121.8 49.4 %all-gather.36.cloned.1.call-done = bf16[512,3,768]{2,0,1:T(8,128)(2,1)} async-done(((bf16[128,3,768]{2,0,1:T(8,128)(2,1)}), bf16[512,3,768]{2,0,1:T(8,128)(2,1)}) %all-gather.36.cloned.1.call-update) | async-done | bytes 2359312 | tf_op jit(solution)/shard_map/all_gather | solution.py:226
  1171.2 8.6 fusion.197
  1181.2 3.5 convolution_convert_fusion.2
  1184.8 46.8 %reduce-scatter.45.cloned.1.call-done = bf16[128,3,768]{2,0,1:T(8,128)(2,1)} async-done(((bf16[512,3,768]{2,0,1:T(8,128)(2,1)}), bf16[128,3,768]{2,0,1:T(8,128)(2,1)}) %reduce-scatter.45.cloned.1.call-update) | async-done | bytes 589840 | tf_op jit(solution)/shard_map/reduce_scatter | solution.py:248
  1236.5 3.6 convolution_bitcast_fusion.6
  1240.1 4.7 fusion.117
  1244.8 4.2 copy.168
  1249.0 4.7 reshape.353
  1256.4 5.8 convolution_bitcast_fusion.4
  1262.3 5.9 convolution_bitcast_fusion.5
  1268.9 7.1 convolution_bitcast_fusion.2
  1276.7 7.1 convolution_bitcast_fusion.3
  1289.8 3.6 convolution_bitcast_fusion.7
  1295.0 70.0 %while.55 = (s32[]{:T(128)}, f32[9,512,64]{1,2,0:T(8,128)}, bf16[9,512,64]{1,2,0:T(8,128)(2,1)S(1)}, f32[9,512,64]{1,2,0:T(8,128)S(1)}, bf16[9,512,64]{2,1,0:T(8...) while((s32[]{:T(128)}, f32[9,512,64]{1,2,0:T(8,128)}, ...), condition=%wide.region_34.35_spmd, body=%wide.region_32.34_spmd.sunk | while | flops 170458624 | bytes 9190513 | solution.py:268
  1367.8 2.8 fusion.114
  1370.7 4.2 copy.166
  1374.9 4.7 reshape.351
  1380.7 4.8 bitcast_convert_fusion
  1392.6 76.8 %reduce-scatter.65.cloned.1.call-done = f32[96,2]{1,0:T(8,128)} async-done(((f32[3072,2]{1,0:T(8,128)}), f32[96,2]{1,0:T(8,128)}) %reduce-scatter.65.cloned.1.call-update) | async-done | bytes 784
  1470.8 43.7 %reduce-scatter.51.cloned.1.call-done = f32[96,768]{1,0:T(8,128)} async-done(((f32[768,768]{1,0:T(8,128)}), f32[96,768]{1,0:T(8,128)}) %reduce-scatter.51.cloned.1.call-update) | async-done | bytes 294928 | tf_op jit(solution)/shard_map/reduce_scatter | solution.py:305
  1514.5 45.8 %reduce-scatter.49.cloned.1.call-done = f32[96,768]{1,0:T(8,128)} async-done(((f32[768,768]{1,0:T(8,128)}), f32[96,768]{1,0:T(8,128)}) %reduce-scatter.49.cloned.1.call-update) | async-done | bytes 294928 | tf_op jit(solution)/shard_map/reduce_scatter | solution.py:305
  1562.2 44.2 %reduce-scatter.55.cloned.1.call-done = f32[768,96]{0,1:T(8,128)} async-done(((f32[768,768]{0,1:T(8,128)}), f32[768,96]{0,1:T(8,128)}) %reduce-scatter.55.cloned.1.call-update) | async-done | bytes 294928 | tf_op jit(solution)/shard_map/reduce_scatter | solution.py:306
  1606.4 45.7 %reduce-scatter.53.cloned.1.call-done = f32[768,96]{0,1:T(8,128)} async-done(((f32[768,768]{0,1:T(8,128)}), f32[768,96]{0,1:T(8,128)}) %reduce-scatter.53.cloned.1.call-update) | async-done | bytes 294928 | tf_op jit(solution)/shard_map/reduce_scatter | solution.py:306
  1657.3 33.1 %reduce-scatter.61.cloned.1.call-done = f32[96,192]{1,0:T(8,128)} async-done(((f32[768,192]{1,0:T(8,128)}), f32[96,192]{1,0:T(8,128)}) %reduce-scatter.61.cloned.1.call-update) | async-done | bytes 73744
  1692.1 42.3 %reduce-scatter.57.cloned.1.call-done = f32[96,576]{1,0:T(8,128)} async-done(((f32[768,576]{1,0:T(8,128)}), f32[96,576]{1,0:T(8,128)}) %reduce-scatter.57.cloned.1.call-update) | async-done | bytes 221200
  1737.0 47.4 %reduce-scatter.47.cloned.1.call-done = bf16[128,3,768]{2,0,1:T(8,128)(2,1)} async-done(((bf16[512,3,768]{2,0,1:T(8,128)(2,1)}), bf16[128,3,768]{2,0,1:T(8,128)(2,1)}) %reduce-scatter.47.cloned.1.call-update) | async-done | bytes 589840 | tf_op jit(solution)/shard_map/reduce_scatter | solution.py:290
  1786.3 40.5 %all-reduce.5 = (f32[2,2,768]{2,1,0:T(2,128)S(1)}, f32[2,2,768]{2,1,0:T(2,128)S(1)}, f32[2,2,768]{2,1,0:T(2,128)S(1)}, f32[2,768]{1,0:T(2,128)S(1)}, f32[2,768]{1,0:T(2,128)S(1)}) all-reduce(f32[2,2,768]{2,1,0:T(2,128)S(1)} %pad_maximum_fusion.11, ...), channel_id=18, replica_groups=mesh['dp'=8,'tensor'=4] {'dp','tensor'}, use_global_device_ids=true, to_apply=%region_42.43.clone | all-reduce | flops 12288 | bytes 98304
  (628 shorter events, 332.8 us)
Async XLA Ops:
  8.0 265.4 %all-gather.24.cloned.1.call-start = ((), (), s32[]{:S(2)}) async-start(), calls=%async_computation.17 | async-start | bytes 2949120 | tf_op jit(solution)/shard_map/all_gather | solution.py:140
  9.3 161.4 %copy-start.44 = (f32[128,3]{0,1:T(4,128)}, f32[128,3]{0,1:T(4,128)S(1)}, u32[]{:S(2)}) copy-start(f32[128,3]{0,1:T(4,128)S(1)} %broadcast_multiply_fusion.11) | copy-start | bytes 4612
  10.7 160.0 %copy-start.50 = (f32[128,3]{0,1:T(4,128)}, f32[128,3]{0,1:T(4,128)S(1)}, u32[]{:S(2)}) copy-start(f32[128,3]{0,1:T(4,128)S(1)} %add_rsqrt_fusion.3) | copy-start | bytes 4612
  160.4 10.2 copy-start.40
  160.4 10.2 copy-start
  171.8 209.7 %reduce-scatter.33.cloned.1.call-start = ((), (), s32[]{:S(2)}) async-start(), calls=%async_computation.18 | async-start | bytes 2949120 | tf_op jit(solution)/shard_map/reduce_scatter | solution.py:153
  313.2 137.6 %all-gather.40.cloned.1.call-start = ((), (), s32[]{:S(2)}) async-start(), calls=%async_computation.37 | async-start | bytes 1327104 | tf_op jit(solution)/shard_map/all_gather | solution.py:96
  314.8 135.9 %all-gather.26.cloned.1.call-start = ((), (), s32[]{:S(2)}) async-start(), calls=%async_computation.19 | async-start | bytes 2949120 | tf_op jit(solution)/shard_map/all_gather | solution.py:162
  384.6 72.8 %all-gather.42.cloned.1.call-start = ((), (), s32[]{:S(2)}) async-start(), calls=%async_computation.38 | async-start | bytes 1327104 | tf_op jit(solution)/shard_map/all_gather | solution.py:97
  385.4 149.3 %reduce-scatter.35.cloned.1.call-start = ((), (), s32[]{:S(2)}) async-start(), calls=%async_computation.20 | async-start | bytes 2949120 | tf_op jit(solution)/shard_map/reduce_scatter | solution.py:174
  450.7 6.7 copy-start.75
  464.7 121.3 %all-gather.28.cloned.1.call-start = ((), (), s32[]{:S(2)}) async-start(), calls=%async_computation.21 | async-start | bytes 2949120 | tf_op jit(solution)/shard_map/all_gather | solution.py:140
  538.0 149.4 %reduce-scatter.37.cloned.1.call-start = ((), (), s32[]{:S(2)}) async-start(), calls=%async_computation.22 | async-start | bytes 2949120 | tf_op jit(solution)/shard_map/reduce_scatter | solution.py:153
  569.8 19.3 %copy-start.25 = (bf16[1,3,768,192]{2,3,1,0:T(8,128)(2,1)}, bf16[1,3,768,192]{2,3,1,0:T(8,128)(2,1)S(1)}, u32[]{:S(2)}) copy-start(bf16[1,3,768,192]{2,3,1,0:T(8,128)(2,1)S(1)} %copy.140) | copy-start | bytes 2654212
  636.5 3.8 copy-start.8
  640.3 47.1 %copy-start.62 = (f32[768]{0:T(1024)S(1)}, f32[768]{0:T(1024)}, u32[]{:S(2)}) copy-start(f32[768]{0:T(1024)} %get-tuple-element.272) | copy-start | bytes 9220
  640.3 53.0 %all-gather.44.cloned.1.call-start = ((), (), s32[]{:S(2)}) async-start(), calls=%async_computation.39 | async-start | bytes 1327104 | tf_op jit(solution)/shard_map/all_gather | solution.py:96
  641.1 99.2 %all-gather.30.cloned.1.call-start = ((), (), s32[]{:S(2)}) async-start(), calls=%async_computation.23 | async-start | bytes 2949120 | tf_op jit(solution)/shard_map/all_gather | solution.py:162
  690.6 73.9 %all-gather.46.cloned.1.call-start = ((), (), s32[]{:S(2)}) async-start(), calls=%async_computation.40 | async-start | bytes 1327104 | tf_op jit(solution)/shard_map/all_gather | solution.py:97
  691.2 124.8 %all-gather.32.cloned.1.call-start = ((), (), s32[]{:S(2)}) async-start(), calls=%async_computation.25 | async-start | bytes 2949120 | tf_op jit(solution)/shard_map/all_gather | solution.py:226
  691.8 184.7 %reduce-scatter.41.cloned.1.call-start = ((), (), s32[]{:S(2)}) async-start(), calls=%async_computation.26 | async-start | bytes 2949120 | tf_op jit(solution)/shard_map/reduce_scatter | solution.py:248
  816.0 10.2 copy-start.89
  829.7 96.6 %reduce-scatter.39.cloned.1.call-start = ((), (), s32[]{:S(2)}) async-start(), calls=%async_computation.24 | async-start | bytes 2949120 | tf_op jit(solution)/shard_map/reduce_scatter | solution.py:174
  837.0 144.3 %all-gather.34.cloned.1.call-start = ((), (), s32[]{:S(2)}) async-start(), calls=%async_computation.27 | async-start | bytes 2949120 | tf_op jit(solution)/shard_map/all_gather | solution.py:261
  931.7 49.6 %copy-start.21 = (bf16[1,192,768]{2,1,0:T(8,128)(2,1)S(1)}, bf16[1,192,768]{2,1,0:T(8,128)(2,1)}, u32[]{:S(2)}) copy-start(bf16[1,192,768]{2,1,0:T(8,128)(2,1)} %copy.145) | copy-start | bytes 884740
  931.7 184.3 %reduce-scatter.43.cloned.1.call-start = ((), (), s32[]{:S(2)}) async-start(), calls=%async_computation.28 | async-start | bytes 2949120 | tf_op jit(solution)/shard_map/reduce_scatter | solution.py:290
  1069.2 46.9 %copy-start.43 = (f32[768]{0:T(1024)S(1)}, f32[768]{0:T(1024)}, u32[]{:S(2)}) copy-start(f32[768]{0:T(1024)} %get-tuple-element.255) | copy-start | bytes 9220
  1069.2 46.9 %copy-start.49 = (f32[128,3]{0,1:T(4,128)S(1)}, f32[128,3]{0,1:T(4,128)}, u32[]{:S(2)}) copy-start(f32[128,3]{0,1:T(4,128)} %copy-done.48) | copy-start | bytes 4612
  1069.2 46.9 %copy-start.55 = (f32[128,3]{0,1:T(4,128)S(1)}, f32[128,3]{0,1:T(4,128)}, u32[]{:S(2)}) copy-start(f32[128,3]{0,1:T(4,128)} %copy-done.54) | copy-start | bytes 4612
  1069.2 102.0 %all-gather.36.cloned.1.call-start = ((), (), s32[]{:S(2)}) async-start(), calls=%async_computation.29 | async-start | bytes 2949120 | tf_op jit(solution)/shard_map/all_gather | solution.py:226
  1120.7 50.5 %copy-start.76 = (f32[768]{0:T(1024)S(1)}, f32[768]{0:T(1024)}, u32[]{:S(2)}) copy-start(f32[768]{0:T(1024)} %copy-done.75) | copy-start | bytes 9220
  1121.6 59.6 %copy-start.88 = (bf16[1,768,768]{2,1,0:T(8,128)(2,1)S(1)}, bf16[1,768,768]{2,1,0:T(8,128)(2,1)}, u32[]{:S(2)}) copy-start(bf16[1,768,768]{2,1,0:T(8,128)(2,1)} %all-gather.40.cloned.1.call-done) | copy-start | bytes 3538948
  1121.6 110.0 %reduce-scatter.45.cloned.1.call-start = ((), (), s32[]{:S(2)}) async-start(), calls=%async_computation.30 | async-start | bytes 2949120 | tf_op jit(solution)/shard_map/reduce_scatter | solution.py:248
  1184.7 46.9 %copy-start.47 = (f32[128,3]{0,1:T(4,128)S(1)}, f32[128,3]{0,1:T(4,128)}, u32[]{:S(2)}) copy-start(f32[128,3]{0,1:T(4,128)} %copy-done.46) | copy-start | bytes 4612
  1184.7 46.9 %copy-start.53 = (f32[128,3]{0,1:T(4,128)S(1)}, f32[128,3]{0,1:T(4,128)}, u32[]{:S(2)}) copy-start(f32[128,3]{0,1:T(4,128)} %copy-done.52) | copy-start | bytes 4612
  1184.7 101.0 %all-gather.38.cloned.1.call-start = ((), (), s32[]{:S(2)}) async-start(), calls=%async_computation.31 | async-start | bytes 2949120 | tf_op jit(solution)/shard_map/all_gather | solution.py:261
  1236.1 4.0 copy-start.28
  1236.1 4.0 copy-start.30
  1236.1 152.2 %reduce-scatter.63.cloned.1.call-start = ((), (), s32[]{:S(2)}) async-start(), calls=%async_computation.44 | async-start | bytes 884736
  1240.1 149.2 %reduce-scatter.59.cloned.1.call-start = ((), (), s32[]{:S(2)}) async-start(), calls=%async_computation.42 | async-start | bytes 2211840
  1253.7 215.6 %reduce-scatter.65.cloned.1.call-start = ((), (), s32[]{:S(2)}) async-start(), calls=%async_computation.45 | async-start | bytes 1622016
  1256.2 258.3 %reduce-scatter.51.cloned.1.call-start = ((), (), s32[]{:S(2)}) async-start(), calls=%async_computation.34 | async-start | bytes 2654208 | tf_op jit(solution)/shard_map/reduce_scatter | solution.py:305
  1262.3 298.0 %reduce-scatter.49.cloned.1.call-start = ((), (), s32[]{:S(2)}) async-start(), calls=%async_computation.33 | async-start | bytes 2654208 | tf_op jit(solution)/shard_map/reduce_scatter | solution.py:305
  1268.2 338.1 %reduce-scatter.55.cloned.1.call-start = ((), (), s32[]{:S(2)}) async-start(), calls=%async_computation.36 | async-start | bytes 2654208 | tf_op jit(solution)/shard_map/reduce_scatter | solution.py:306
  1276.0 376.1 %reduce-scatter.53.cloned.1.call-start = ((), (), s32[]{:S(2)}) async-start(), calls=%async_computation.35 | async-start | bytes 2654208 | tf_op jit(solution)/shard_map/reduce_scatter | solution.py:306
  1283.8 406.6 %reduce-scatter.61.cloned.1.call-start = ((), (), s32[]{:S(2)}) async-start(), calls=%async_computation.43 | async-start | bytes 884736
  1293.4 441.1 %reduce-scatter.57.cloned.1.call-start = ((), (), s32[]{:S(2)}) async-start(), calls=%async_computation.41 | async-start | bytes 2211840
  1379.6 404.8 %reduce-scatter.47.cloned.1.call-start = ((), (), s32[]{:S(2)}) async-start(), calls=%async_computation.32 | async-start | bytes 2949120 | tf_op jit(solution)/shard_map/reduce_scatter | solution.py:290
  1387.8 3.5 copy-start.68
  1387.8 3.5 copy-start.72
  1387.8 3.5 copy-start.67
  1560.3 93.9 %copy-start.70 = (f32[768]{0:T(1024)S(1)}, f32[768]{0:T(1024)}, u32[]{:S(2)}) copy-start(f32[768]{0:T(1024)} %get-tuple-element.246) | copy-start | bytes 9220
  1560.3 94.5 %copy-start.71 = (f32[768]{0:T(1024)S(1)}, f32[768]{0:T(1024)}, u32[]{:S(2)}) copy-start(f32[768]{0:T(1024)} %get-tuple-element.341) | copy-start | bytes 9220
  1560.3 94.5 %copy-start.69 = (f32[768]{0:T(1024)S(1)}, f32[768]{0:T(1024)}, u32[]{:S(2)}) copy-start(f32[768]{0:T(1024)} %get-tuple-element.267) | copy-start | bytes 9220
  1652.1 4.7 copy-start.5
  1657.0 78.8 %copy-start.22 = (f32[3,96,192]{1,2,0:T(8,128)S(1)}, f32[3,96,192]{1,2,0:T(8,128)}, u32[]{:S(2)}) copy-start(f32[3,96,192]{1,2,0:T(8,128)} %copy.169) | copy-start | bytes 663556
  1735.8 48.6 %copy-start.41 = (f32[768]{0:T(1024)S(1)}, f32[768]{0:T(1024)}, u32[]{:S(2)}) copy-start(f32[768]{0:T(1024)} %copy-done.40) | copy-start | bytes 9220
  1735.8 48.6 %copy-start.45 = (f32[128,3]{0,1:T(4,128)S(1)}, f32[128,3]{0,1:T(4,128)}, u32[]{:S(2)}) copy-start(f32[128,3]{0,1:T(4,128)} %copy-done.44) | copy-start | bytes 4612
  1735.8 48.6 %copy-start.51 = (f32[128,3]{0,1:T(4,128)S(1)}, f32[128,3]{0,1:T(4,128)}, u32[]{:S(2)}) copy-start(f32[128,3]{0,1:T(4,128)} %copy-done.50) | copy-start | bytes 4612
  1735.8 50.4 %copy-start.73 = (f32[1,768]{1,0:T(1,128)S(1)}, f32[1,768]{1,0:T(1,128)}, u32[]{:S(2)}) copy-start(f32[1,768]{1,0:T(1,128)} %stack.159) | copy-start | bytes 9220
  1735.8 50.4 %copy-start.57 = (f32[1,2,768]{2,1,0:T(2,128)S(1)}, f32[1,2,768]{2,1,0:T(2,128)}, u32[]{:S(2)}) copy-start(f32[1,2,768]{2,1,0:T(2,128)} %maximum_bitcast_fusion.1) | copy-start | bytes 18436
  1735.9 50.4 %copy-start.74 = (f32[1,768]{1,0:T(1,128)S(1)}, f32[1,768]{1,0:T(1,128)}, u32[]{:S(2)}) copy-start(f32[1,768]{1,0:T(1,128)} %stack.168) | copy-start | bytes 9220
  1735.9 50.4 %copy-start.58 = (f32[1,2,768]{2,1,0:T(2,128)S(1)}, f32[1,2,768]{2,1,0:T(2,128)}, u32[]{:S(2)}) copy-start(f32[1,2,768]{2,1,0:T(2,128)} %maximum_bitcast_fusion.3) | copy-start | bytes 18436
  1784.4 45.7 %copy-start.19 = (bf16[128,3,768]{2,0,1:T(8,128)(2,1)S(1)}, bf16[128,3,768]{2,0,1:T(8,128)(2,1)}, u32[]{:S(2)}) copy-start(bf16[128,3,768]{2,0,1:T(8,128)(2,1)} %reduce-scatter.47.cloned.1.call-done) | copy-start | bytes 1769476
  (55 other events, 80.6 us)
Sparse Core Ops, SparseCore 0:
  171.9 52.5 all-gather.23
  313.3 45.6 reduce-scatter.32
  538.1 47.7 all-gather.27
  640.5 46.8 reduce-scatter.36
  829.8 46.6 reduce-scatter.40
  878.7 47.5 reduce-scatter.38
  1069.3 46.6 reduce-scatter.42
  1184.8 46.6 reduce-scatter.44
Sparse Core Ops, SparseCore 1:
  316.1 21.3 all-gather.39
  384.7 48.3 all-gather.25
  434.8 22.6 all-gather.41
  464.7 47.9 reduce-scatter.34
  643.6 22.7 all-gather.43
  690.7 49.5 all-gather.29
  742.0 22.5 all-gather.45
  766.0 50.0 all-gather.31
  931.8 49.5 all-gather.33
  1121.6 49.5 all-gather.35
  1236.2 49.5 all-gather.37
  1288.9 33.6 reduce-scatter.62
  1325.9 40.2 reduce-scatter.58
  1372.3 97.1 reduce-scatter.64
  1473.1 41.3 reduce-scatter.50
  1517.9 42.3 reduce-scatter.48
  1564.0 42.3 reduce-scatter.54
  1609.8 42.3 reduce-scatter.52
  1655.5 34.9 reduce-scatter.60
  1694.2 40.2 reduce-scatter.56
  1736.6 47.7 reduce-scatter.46
where the time goes:
time: 1850 us; the launch traced here: 1840 us
  waiting for transfers between devices  839 us (45%)
  blocking collectives  497 us (27%)
  matrix products  280 us (15%)
  local copies, waits for them, and re-layouts  144 us (8%)
  other arithmetic  58.2 us (3%)
    unnamed x34, waiting for transfers between devices  155 us
    all_gather x2, waiting for transfers between devices, on_device(): lax.all_gather(upstream.astype(jnp.bfloat16), 'tensor', axis=0, tiled=True)  101 us
    reduce_scatter x2, waiting for transfers between devices, on_device(): lax.psum_scatter(row_products('lsce,cde->lsd', grad_projected, layer_para...  94.2 us
    reduce_scatter x2, waiting for transfers between devices, on_device(): lax.psum_scatter(contract_grad, 'dp', scatter_dimension=1, tiled=True)  89.9 us
    reduce_scatter x2, waiting for transfers between devices, on_device(): lax.psum_scatter(expand_grad, 'dp', scatter_dimension=0, tiled=True)  89.4 us
    reduce_scatter x2, waiting for transfers between devices, on_device(): lax.psum_scatter(row_products('xgj,oj->xgo', hidden_gradient_reduced, lay...  85.9 us
    all_gather x1, blocking collectives, on_device(): lax.all_gather(norm_shift, ('dp', 'tensor'), axis=2, tiled=True)  72.8 us
    all_gather x1, blocking collectives, on_device(): lax.all_gather(attention_bias, ('dp', 'tensor'), axis=2, tiled=True)  72.1 us
  transfers between devices with their start and end apart: 29, of which 21 were waited for; matrix products, arithmetic and copies ran while one was open for 11% of the time, Pallas kernels for 0%

commit v1 on v0

v1 whole, which is shorter than its diff:
```python
import functools

import jax
import jax.numpy as jnp
from jax import lax
from jax.experimental import pallas as pl
from jax.experimental.pallas import tpu as pltpu
from jax.sharding import PartitionSpec as P

HEAD = 64
EPSILON = 1e-05
ROWS = 256
F32 = jnp.float32
BF16 = jnp.bfloat16


def norm_stats(rows):
    average = jnp.mean(rows, axis=-1, keepdims=True)
    centred = rows - average
    inverse = lax.rsqrt(jnp.mean(centred * centred, axis=-1, keepdims=True) + EPSILON)
    return (centred * inverse, inverse)


def norm_back(incoming, gain, scaled, inverse):
    weighted = incoming * gain
    first = jnp.mean(weighted, axis=-1, keepdims=True)
    second = jnp.mean(weighted * scaled, axis=-1, keepdims=True)
    return inverse * (weighted - first - scaled * second)


def smooth_unit(values):
    return jax.nn.gelu(values, approximate=True)


def dot(left, right, contract):
    return lax.dot_general(left, right, (contract, ((), ())), preferred_element_type=F32)


def block_probs(query, keys, start):
    scores = dot(query, keys, ((1,), (1,)))
    later = lax.broadcasted_iota(jnp.int32, scores.shape, 0) + start
    earlier = lax.broadcasted_iota(jnp.int32, scores.shape, 1)
    scores = jnp.where(later >= earlier, scores, -1e30)
    powers = jnp.exp(scores - jnp.max(scores, axis=-1, keepdims=True))
    return powers / jnp.sum(powers, axis=-1, keepdims=True)


def attend_kernel(qkv_ref, context_ref):
    length = qkv_ref.shape[1]
    for start in range(0, length, ROWS):
        stop = start + ROWS
        parts = []
        for head in range(2):
            lanes = slice(head * HEAD, (head + 1) * HEAD)
            query = qkv_ref[0, start:stop, lanes] * BF16(HEAD**-0.5)
            probs = block_probs(query, qkv_ref[1, :stop, lanes], start)
            parts.append(dot(probs.astype(BF16), qkv_ref[2, :stop, lanes], ((1,), (0,))))
        context_ref[start:stop, :] = jnp.concatenate(parts, axis=1).astype(BF16)


def attend_back_kernel(qkv_ref, up_ref, grad_ref, bias_ref, total_ref):
    length = qkv_ref.shape[1]
    total_ref[...] = jnp.zeros_like(total_ref)
    bias = jnp.zeros((1, 2 * HEAD), F32)
    for start in range(0, length, ROWS):
        stop = start + ROWS
        parts = []
        for head in range(2):
            lanes = slice(head * HEAD, (head + 1) * HEAD)
            query = qkv_ref[0, start:stop, lanes] * BF16(HEAD**-0.5)
            keys = qkv_ref[1, :stop, lanes]
            values = qkv_ref[2, :stop, lanes]
            upstream = up_ref[start:stop, lanes]
            probs = block_probs(query, keys, start)
            grad_probs = dot(upstream, values, ((1,), (1,)))
            inner = jnp.sum(grad_probs * probs, axis=-1, keepdims=True)
            grad_scores = (probs * (grad_probs - inner)).astype(BF16)
            parts.append(dot(grad_scores, keys, ((1,), (0,))) * (HEAD**-0.5))
            total_ref[0, :stop, lanes] += dot(grad_scores, query, ((0,), (0,)))
            total_ref[1, :stop, lanes] += dot(probs.astype(BF16), upstream, ((0,), (0,)))
        grad_query = jnp.concatenate(parts, axis=1)
        bias = bias + jnp.sum(grad_query, axis=0, keepdims=True)
        grad_ref[0, start:stop, :] = grad_query.astype(BF16)
    grad_ref[1] = total_ref[0].astype(BF16)
    grad_ref[2] = total_ref[1].astype(BF16)
    bias_ref[0] = jnp.broadcast_to(bias, bias_ref.shape[1:])
    bias_ref[1] = jnp.broadcast_to(
        jnp.sum(total_ref[1], axis=0, keepdims=True), bias_ref.shape[1:]
    )


def attend(qkv):
    unused, length, width = qkv.shape
    return pl.pallas_call(
        attend_kernel,
        grid=(width // 128,),
        in_specs=[pl.BlockSpec((3, length, 128), lambda pair: (0, 0, pair))],
        out_specs=pl.BlockSpec((length, 128), lambda pair: (0, pair)),
        out_shape=jax.ShapeDtypeStruct((length, width), BF16),
        compiler_params=pltpu.CompilerParams(vmem_limit_bytes=32 << 20),
        cost_estimate=pl.CostEstimate(
            flops=4 * length * length * width,
            bytes_accessed=8 * length * width,
            transcendentals=length * length * width // HEAD,
        ),
    )(qkv)


def attend_back(qkv, upstream):
    unused, length, width = qkv.shape
    grads, bias = pl.pallas_call(
        attend_back_kernel,
        grid=(width // 128,),
        in_specs=[
            pl.BlockSpec((3, length, 128), lambda pair: (0, 0, pair)),
            pl.BlockSpec((length, 128), lambda pair: (0, pair)),
        ],
        out_specs=(
            pl.BlockSpec((3, length, 128), lambda pair: (0, 0, pair)),
            pl.BlockSpec((2, 8, 128), lambda pair: (0, 0, pair)),
        ),
        out_shape=(
            jax.ShapeDtypeStruct((3, length, width), BF16),
            jax.ShapeDtypeStruct((2, 8, width), F32),
        ),
        scratch_shapes=[pltpu.VMEM((2, length, 128), F32)],
        compiler_params=pltpu.CompilerParams(vmem_limit_bytes=32 << 20),
        cost_estimate=pl.CostEstimate(
            flops=10 * length * length * width,
            bytes_accessed=14 * length * width,
            transcendentals=length * length * width // HEAD,
        ),
    )(qkv, upstream)
    return grads, bias[:, 0]


def to_sequences(rows):
    devices = lax.axis_size("tensor")
    items = rows.transpose(1, 0, 2)
    items = jnp.pad(items, ((0, devices - items.shape[0]), (0, 0), (0, 0)))
    items = lax.all_to_all(items, "tensor", split_axis=0, concat_axis=0, tiled=True)
    return items.reshape(-1, rows.shape[2])


def to_positions(rows, sequences):
    devices = lax.axis_size("tensor")
    items = rows.reshape(devices, -1, rows.shape[1])
    items = lax.all_to_all(items, "tensor", split_axis=0, concat_axis=0, tiled=True)
    return items[:sequences].transpose(1, 0, 2)


def gather(weight, split, head):
    weight = lax.all_gather(weight, "tensor", axis=head, tiled=True)
    return lax.all_gather(weight, "dp", axis=split, tiled=True)


def scatter(grad, split, head):
    grad = lax.psum_scatter(grad.astype(BF16), "dp", scatter_dimension=split, tiled=True)
    grad = lax.psum_scatter(grad, "tensor", scatter_dimension=head, tiled=True)
    return grad.astype(F32)


def on_device(
    inputs,
    cotangent,
    norm_gain,
    norm_shift,
    attention_weight,
    attention_bias,
    output_weight,
    output_bias,
    expand_weight,
    expand_bias,
    contract_weight,
    contract_bias,
):
    sequences = inputs.shape[1]
    layers = attention_weight.shape[0]
    both = ("dp", "tensor")
    small = (norm_gain, norm_shift, attention_bias, output_bias, expand_bias, contract_bias)
    packed = jnp.concatenate([item.reshape(-1) for item in small])
    packed = lax.all_gather(packed, both, axis=0, tiled=False).astype(F32)
    shared = []
    start = 0
    for item in small:
        part = packed[:, start : start + item.size].reshape((-1,) + item.shape)
        shared.append(jnp.moveaxis(part, 0, -2).reshape(item.shape[:-1] + (-1,)))
        start += item.size
    gains, shifts, attention_shift, output_shift, expand_shift, contract_shift = shared
    weights = []
    for layer in range(layers):
        weights.append(
            (
                gather(attention_weight[layer], 1, 2),
                gather(output_weight[layer], 1, 0),
                gather(expand_weight[layer], 0, 1),
                gather(contract_weight[layer], 1, 0),
            )
        )
    residual = to_sequences(inputs).astype(F32)
    width = residual.shape[1]
    stored = []
    for layer in range(layers):
        attention, output, expand, contract = weights[layer]
        scaled, inverse = norm_stats(residual)
        normed = (scaled * gains[layer, 0] + shifts[layer, 0]).astype(BF16)
        shift = jnp.stack(
            [attention_shift[layer, 0], jnp.zeros((width,), F32), attention_shift[layer, 1]]
        )
        qkv = jnp.einsum("ld,cde->cle", normed, attention, preferred_element_type=F32)
        qkv = (qkv + shift[:, None]).astype(BF16)
        context = attend(qkv)
        middle = residual + dot(context, output, ((1,), (0,))) + output_shift[layer]
        scaled, inverse = norm_stats(middle)
        expanded = (scaled * gains[layer, 1] + shifts[layer, 1]).astype(BF16)
        hidden = dot(expanded, expand, ((1,), (0,))) + expand_shift[layer]
        active = smooth_unit(hidden).astype(BF16)
        stored.append((residual, normed, qkv, context, middle, expanded, hidden, active))
        residual = middle + dot(active, contract, ((1,), (0,))) + contract_shift[layer]
    outputs = to_positions(residual.astype(BF16), sequences)
    upstream = to_sequences(cotangent).astype(F32)
    weight_parts = []
    small_parts = []
    for layer in reversed(range(layers)):
        attention, output, expand, contract = weights[layer]
        before, normed, qkv, context, middle, expanded, hidden, active = stored[layer]
        contract_bias_grad = jnp.sum(upstream, axis=0)
        upstream_low = upstream.astype(BF16)
        contract_grad = scatter(dot(active, upstream_low, ((0,), (0,))), 1, 0)
        grad_active = dot(upstream_low, contract, ((1,), (1,)))
        unused, pull_unit = jax.vjp(smooth_unit, hidden)
        grad_hidden = pull_unit(grad_active)[0]
        expand_bias_grad = jnp.sum(grad_hidden, axis=0)
        hidden_low = grad_hidden.astype(BF16)
        expand_grad = scatter(dot(expanded, hidden_low, ((0,), (0,))), 0, 1)
        grad_second = dot(hidden_low, expand, ((1,), (1,)))
        scaled, inverse = norm_stats(middle)
        second_gain = jnp.sum(grad_second * scaled, axis=0)
        second_shift = jnp.sum(grad_second, axis=0)
        grad_middle = upstream + norm_back(grad_second, gains[layer, 1], scaled, inverse)
        output_bias_grad = jnp.sum(grad_middle, axis=0)
        middle_low = grad_middle.astype(BF16)
        output_grad = scatter(dot(context, middle_low, ((0,), (0,))), 1, 0)
        grad_context = dot(middle_low, output, ((1,), (1,))).astype(BF16)
        grad_qkv, attention_bias_grad = attend_back(qkv, grad_context)
        attention_grad = scatter(
            jnp.einsum("ld,cle->cde", normed, grad_qkv, preferred_element_type=F32), 1, 2
        )
        grad_first = jnp.einsum("cle,cde->ld", grad_qkv, attention, preferred_element_type=F32)
        scaled, inverse = norm_stats(before)
        first_gain = jnp.sum(grad_first * scaled, axis=0)
        first_shift = jnp.sum(grad_first, axis=0)
        upstream = grad_middle + norm_back(grad_first, gains[layer, 0], scaled, inverse)
        weight_parts.insert(0, (attention_grad, output_grad, expand_grad, contract_grad))
        small_parts.insert(
            0,
            (
                jnp.stack([first_gain, second_gain]),
                jnp.stack([first_shift, second_shift]),
                attention_bias_grad,
                output_bias_grad,
                expand_bias_grad,
                contract_bias_grad,
            ),
        )
    first_input_grad = to_positions(upstream.astype(BF16), sequences).astype(F32)
    pieces = []
    for index, item in enumerate(small):
        grad = jnp.stack([parts[index] for parts in small_parts])
        grad = grad.reshape(item.shape[:-1] + (-1, item.shape[-1]))
        pieces.append(jnp.moveaxis(grad, -2, 0).reshape(-1, item.size))
    packed = jnp.concatenate(pieces, axis=1)
    packed = lax.psum_scatter(packed, both, scatter_dimension=0, tiled=True)[0]
    small_out = []
    start = 0
    for item in small:
        small_out.append(packed[start : start + item.size].reshape(item.shape))
        start += item.size
    large = [jnp.stack([parts[index] for parts in weight_parts]) for index in range(4)]
    return (
        outputs,
        first_input_grad,
        small_out[0],
        small_out[1],
        large[0],
        small_out[2],
        large[1],
        small_out[3],
        large[2],
        small_out[4],
        large[3],
        small_out[5],
    )


def solution(mesh):
    return jax.shard_map(
        on_device,
        mesh=mesh,
        in_specs=(
            P("tensor", "dp", None),
            P("tensor", "dp", None),
            P(None, None, ("dp", "tensor")),
            P(None, None, ("dp", "tensor")),
            P(None, None, "dp", "tensor"),
            P(None, None, ("dp", "tensor")),
            P(None, "tensor", "dp"),
            P(None, ("dp", "tensor")),
            P(None, "dp", "tensor"),
            P(None, ("dp", "tensor")),
            P(None, "tensor", "dp"),
            P(None, ("dp", "tensor")),
        ),
        out_specs=(
            P("tensor", "dp", None),
            P("tensor", "dp", None),
            P(None, None, ("dp", "tensor")),
            P(None, None, ("dp", "tensor")),
            P(None, None, "dp", "tensor"),
            P(None, None, ("dp", "tensor")),
            P(None, "tensor", "dp"),
            P(None, ("dp", "tensor")),
            P(None, "dp", "tensor"),
            P(None, ("dp", "tensor")),
            P(None, "tensor", "dp"),
            P(None, ("dp", "tensor")),
        ),
        check_vma=False,
    )
```

time: 1850 us -> 1090 us (0.59)
  blocking collectives: 497 us -> 182 us
  waiting for transfers between devices: 839 us -> 580 us
  matrix products: 280 us -> 132 us
  local copies, waits for them, and re-layouts: 144 us -> 73.3 us
  Pallas kernels: 0 us -> 62.7 us
  other arithmetic: 58.2 us -> 18.1 us
    all_gather x10 -> x8, blocking collectives: 457 us -> 141 us  [gather(): weight = lax.all_gather(weight, 'tensor', axis=head, tiled=True)]
    all_gather x12 -> x8, waiting for transfers between devices: 232 us -> 35.7 us  [gather(): return lax.all_gather(weight, 'dp', axis=split, tiled=True)]
    dot_general x150 -> x24, matrix products: 280 us -> 132 us  [the longest x18 105 us: dot(): lax.dot_general(left, right, (contract, ((), ())), preferred_element_type...]
    reduce_scatter x12, waiting for transfers between devices: 452 us -> 336 us  [the longest x6 205 us: scatter(): lax.psum_scatter(grad.astype(BF16), 'dp', scatter_dimension=split, tiled=...]
    pallas_call x0 -> x4, Pallas kernels: none -> 62.7 us  [the longest x2 38.6 us: attend_back(): pl.pallas_call(attend_back_kernel, grid=(width // 128,), in_specs=[pl.Blo...]
    unnamed x34 -> x30, waiting for transfers between devices: 155 us -> 208 us
    slice x14 -> x23, local copies, waits for them, and re-layouts: 28.9 us -> 4.32 us  [the longest x3 2.44 us: on_device(): small_out.append(packed[start:start + item.size].reshape(item.shape))]
    dynamic_update_slice x22 -> x0, local copies, waits for them, and re-layouts: 24.5 us -> none  [the longest x18 24.2 us: on_device(): lax.map(attend_forward, (split_heads(query), split_heads(keys), split_hea...]
  transfers between devices with their start and end apart: 29 -> 29, of which waited for: 21 -> 16; matrix products, arithmetic and copies ran while one was open for 11% -> 17% of each run, Pallas kernels for 0% -> 4%
where the time goes in v1:
time: 1090 us; the launch traced here: 1080 us
  waiting for transfers between devices  580 us (53%)
  blocking collectives  182 us (17%)
  matrix products  132 us (12%)
  local copies, waits for them, and re-layouts  73.3 us (7%)
  Pallas kernels  62.7 us (6%)
  starting transfers between devices  20.2 us (2%)
  other arithmetic  18.1 us (2%)
  between operations  15.6 us (1%)
    unnamed x30, waiting for transfers between devices  208 us
    reduce_scatter x6, waiting for transfers between devices, scatter(): lax.psum_scatter(grad.astype(BF16), 'dp', scatter_dimension=split, tiled=...  205 us
    all_gather x8, blocking collectives, gather(): weight = lax.all_gather(weight, 'tensor', axis=head, tiled=True)  141 us
    reduce_scatter x6, waiting for transfers between devices, scatter(): grad = lax.psum_scatter(grad, 'tensor', scatter_dimension=head, tiled=True)  131 us
    dot_general x18, matrix products, dot(): lax.dot_general(left, right, (contract, ((), ())), preferred_element_type...  105 us
    unnamed x104, local copies, waits for them, and re-layouts  53.3 us
    unnamed x1, blocking collectives  41 us
    pallas_call x2, Pallas kernels, attend_back(): pl.pallas_call(attend_back_kernel, grid=(width // 128,), in_specs=[pl.Blo...  38.6 us
  transfers between devices with their start and end apart: 29, of which 16 were waited for; matrix products, arithmetic and copies ran while one was open for 17% of the time, Pallas kernels for 4%

profile of v1, /device:TPU:0, one launch (start us, length us, event | category | flops | bytes accessed | tf_op | source)
XLA Modules:
  0.0 1084.1 jit_solution(10820953543176498933)
XLA Ops:
  8.4 21.3 %all-gather.1 = bf16[1,3,96,768]{2,1,0,3:T(4,128)(2,1)S(1)} all-gather(bf16[1,3,96,192]{2,1,0,3:T(4,128)(2,1)S(1)} %copy.137), channel_id=3, replica_groups=mesh['dp'=8,'tensor'=4] {'tensor'}, dimensions={3}, use_global_device_ids=true | all-gather | bytes 552960 | tf_op jit(solution)/shard_map/all_gather | solution.py:153
  31.1 15.2 %all-gather.3 = bf16[1,768,96]{2,0,1:T(2,128)(2,1)S(1)} all-gather(bf16[1,192,96]{2,0,1:T(2,128)(2,1)S(1)} %copy.138), channel_id=5, replica_groups=mesh['dp'=8,'tensor'=4] {'tensor'}, dimensions={1}, use_global_device_ids=true | all-gather | bytes 184320 | tf_op jit(solution)/shard_map/all_gather | solution.py:153
  47.2 17.3 %all-gather.5 = bf16[1,96,3072]{2,1,0:T(8,128)(2,1)} all-gather(bf16[1,96,768]{2,1,0:T(8,128)(2,1)S(1)} %get-tuple-element.116), channel_id=7, replica_groups=mesh['dp'=8,'tensor'=4] {'tensor'}, dimensions={2}, use_global_device_ids=true | all-gather | bytes 737280 | tf_op jit(solution)/shard_map/all_gather | solution.py:153
  64.7 15.8 %all-gather.7 = bf16[1,3072,96]{1,2,0:T(8,128)(2,1)} all-gather(bf16[1,768,96]{1,2,0:T(8,128)(2,1)S(1)} %get-tuple-element.118), channel_id=9, replica_groups=mesh['dp'=8,'tensor'=4] {'tensor'}, dimensions={1}, use_global_device_ids=true | all-gather | bytes 737280 | tf_op jit(solution)/shard_map/all_gather | solution.py:153
  80.7 16.7 %all-gather.9 = bf16[1,3,96,768]{2,1,0,3:T(4,128)(2,1)S(1)} all-gather(bf16[1,3,96,192]{2,1,0,3:T(4,128)(2,1)S(1)} %copy.139), channel_id=11, replica_groups=mesh['dp'=8,'tensor'=4] {'tensor'}, dimensions={3}, use_global_device_ids=true | all-gather | bytes 552960 | tf_op jit(solution)/shard_map/all_gather | solution.py:153
  98.8 15.0 %all-gather.11 = bf16[1,768,96]{2,0,1:T(2,128)(2,1)S(1)} all-gather(bf16[1,192,96]{2,0,1:T(2,128)(2,1)S(1)} %copy.140), channel_id=13, replica_groups=mesh['dp'=8,'tensor'=4] {'tensor'}, dimensions={1}, use_global_device_ids=true | all-gather | bytes 184320 | tf_op jit(solution)/shard_map/all_gather | solution.py:153
  114.7 18.1 %all-gather.13 = bf16[1,96,3072]{2,1,0:T(8,128)(2,1)} all-gather(bf16[1,96,768]{2,1,0:T(8,128)(2,1)S(1)} %get-tuple-element.115), channel_id=15, replica_groups=mesh['dp'=8,'tensor'=4] {'tensor'}, dimensions={2}, use_global_device_ids=true | all-gather | bytes 737280 | tf_op jit(solution)/shard_map/all_gather | solution.py:153
  133.9 5.9 all-to-all-start
  139.8 21.8 %all-gather.15 = bf16[1,3072,96]{1,2,0:T(8,128)(2,1)} all-gather(bf16[1,768,96]{1,2,0:T(8,128)(2,1)S(1)} %get-tuple-element.117), channel_id=17, replica_groups=mesh['dp'=8,'tensor'=4] {'tensor'}, dimensions={1}, use_global_device_ids=true | all-gather | bytes 737280 | tf_op jit(solution)/shard_map/all_gather | solution.py:153
  162.5 41.0 %all-reduce.2 = bf16[18432]{0:T(1024)(128)(2,1)S(1)} all-reduce(bf16[18432]{0:T(1024)(128)(2,1)S(1)} %dynamic-update-slice), channel_id=2, replica_groups=mesh['dp'=8,'tensor'=4] {'dp','tensor'}, use_global_device_ids=true, to_apply=%add.2 | all-reduce | flops 18432 | bytes 73728
  206.7 3.5 all-to-all-start.2
  212.1 4.0 fusion.40.qkv_ref
  216.1 12.0 %shard_map.211 = bf16[512,768]{1,0:T(8,128)(2,1)S(1)} custom-call(bf16[3,512,768]{2,1,0:T(8,128)(2,1)S(1)} %fusion.40.qkv_ref), custom_call_target="tpu_custom_call" | custom-call | flops 805306368 | bytes 3145728 | tf_op jit(solution)/shard_map/pallas_call | solution.py:94
  229.5 2.2 fusion.100
  233.1 8.2 fusion.26
  241.4 9.1 fusion.101
  252.0 4.6 fusion.41.qkv_ref
  256.6 12.1 %shard_map.212 = bf16[512,768]{1,0:T(8,128)(2,1)S(1)} custom-call(bf16[3,512,768]{2,1,0:T(8,128)(2,1)S(1)} %fusion.41.qkv_ref), custom_call_target="tpu_custom_call" | custom-call | flops 805306368 | bytes 3145728 | tf_op jit(solution)/shard_map/pallas_call | solution.py:94
  270.1 2.7 fusion.102
  274.2 3.0 all-gather.38.cloned.1.call-done
  277.2 8.2 fusion.18
  285.4 32.6 %all-gather.40.cloned.1.call-done = bf16[1,3072,768]{1,2,0:T(8,128)(2,1)} async-done(((bf16[1,3072,96]{1,2,0:T(8,128)(2,1)}), bf16[1,3072,768]{1,2,0:T(8,128)(2,1)}) %all-gather.40.cloned.1.call-update) | async-done | bytes 4718608 | tf_op jit(solution)/shard_map/all_gather | solution.py:154
  318.0 9.7 fusion.103
  327.7 3.1 multiply_reduce_fusion
  331.5 1.8 convolution_convert_fusion.4
  333.4 2.2 convolution_convert_fusion.7.up_ref
  335.6 19.5 %shard_map.213 = (bf16[3,512,768]{2,1,0:T(8,128)(2,1)S(1)}, f32[2,8,768]{2,1,0:T(8,128)S(1)}) custom-call(bf16[3,512,768]{2,1,0:T(8,128)(2,1)S(1)} %copy-done.3, bf16[512,768]{1,0:T(8,128)(2,1)S(1)} %convolution_convert_fusion.7.up_ref), custom_call_target="tpu_custom_call" | custom-call | flops 2013265920 | bytes 5505024 | tf_op jit(solution)/shard_map/pallas_call | solution.py:111
  355.1 3.4 fusion.47
  358.6 3.1 fusion.88
  361.7 10.3 fusion.104
  372.1 3.1 multiply_reduce_fusion.1
  377.0 3.3 convolution_convert_fusion.5
  380.5 5.4 convert_bitcast_fusion
  385.9 8.1 copy.131
  394.0 4.9 copy.142
  399.0 2.7 convolution_convert_fusion.6.up_ref
  401.7 19.1 %shard_map.214 = (bf16[3,512,768]{2,1,0:T(8,128)(2,1)S(1)}, f32[2,8,768]{2,1,0:T(8,128)S(1)}) custom-call(bf16[3,512,768]{2,1,0:T(8,128)(2,1)S(1)} %copy-done.1, bf16[512,768]{1,0:T(8,128)(2,1)S(1)} %convolution_convert_fusion.6.up_ref), custom_call_target="tpu_custom_call" | custom-call | flops 2013265920 | bytes 5505024 | tf_op jit(solution)/shard_map/pallas_call | solution.py:111
  422.2 3.8 convert_bitcast_fusion.1
  426.1 8.1 copy.129
  434.2 4.9 copy.141
  440.6 6.5 convolution_convert_fusion.2
  448.6 6.7 convolution_convert_fusion.3
  456.4 8.2 convolution_convert_fusion
  466.0 8.2 convolution_convert_fusion.1
  476.3 5.4 fusion.46
  491.5 47.3 %reduce-scatter.49.cloned.1.call-done = bf16[96,2304]{1,0:T(8,128)(2,1)} async-done(((bf16[768,2304]{1,0:T(8,128)(2,1)}), bf16[96,2304]{1,0:T(8,128)(2,1)}) %reduce-scatter.49.cloned.1.call-update) | async-done | bytes 442384
  541.7 54.5 %reduce-scatter.37.cloned.1.call-done = bf16[96,3072]{1,0:T(8,128)(2,1)} async-done(((bf16[768,3072]{1,0:T(8,128)(2,1)}), bf16[96,3072]{1,0:T(8,128)(2,1)}) %reduce-scatter.37.cloned.1.call-update) | async-done | bytes 589840 | tf_op jit(solution)/shard_map/reduce_scatter | solution.py:158
  596.4 57.4 %reduce-scatter.33.cloned.1.call-done = bf16[96,3072]{1,0:T(8,128)(2,1)} async-done(((bf16[768,3072]{1,0:T(8,128)(2,1)}), bf16[96,3072]{1,0:T(8,128)(2,1)}) %reduce-scatter.33.cloned.1.call-update) | async-done | bytes 589840 | tf_op jit(solution)/shard_map/reduce_scatter | solution.py:158
  653.8 9.1 add_convert_fusion.2
  662.9 4.6 all-to-all-start.1
  667.5 43.5 %reduce-scatter.45.cloned.1.call-done = bf16[3072,96]{0,1:T(8,128)(2,1)} async-done(((bf16[3072,768]{0,1:T(8,128)(2,1)}), bf16[3072,96]{0,1:T(8,128)(2,1)}) %reduce-scatter.45.cloned.1.call-update) | async-done | bytes 589840 | tf_op jit(solution)/shard_map/reduce_scatter | solution.py:158
  711.0 3.3 fusion.60
  714.3 4.6 all-to-all-start.3
  718.9 49.7 %reduce-scatter.41.cloned.1.call-done = bf16[3072,96]{0,1:T(8,128)(2,1)} async-done(((bf16[3072,768]{0,1:T(8,128)(2,1)}), bf16[3072,96]{0,1:T(8,128)(2,1)}) %reduce-scatter.41.cloned.1.call-update) | async-done | bytes 589840 | tf_op jit(solution)/shard_map/reduce_scatter | solution.py:158
  768.6 125.4 %all-reduce.6.cloned.1.call-done = f32[32,576]{1,0:T(8,128)} async-done(((f32[32,576]{1,0:T(8,128)}), f32[32,576]{1,0:T(8,128)}) %all-reduce.6.cloned.1.call-update) | async-done | bytes 73744
  902.4 15.7 %reduce-scatter.55.cloned.1.call-done = bf16[192,96]{1,0:T(8,128)(2,1)} async-done(((bf16[768,96]{1,0:T(8,128)(2,1)}), bf16[192,96]{1,0:T(8,128)(2,1)}) %reduce-scatter.55.cloned.1.call-update) | async-done | bytes 36880
  919.0 19.6 %reduce-scatter.53.cloned.1.call-done = bf16[192,96]{1,0:T(8,128)(2,1)} async-done(((bf16[768,96]{1,0:T(8,128)(2,1)}), bf16[192,96]{1,0:T(8,128)(2,1)}) %reduce-scatter.53.cloned.1.call-update) | async-done | bytes 36880
  940.3 21.2 %reduce-scatter.27.cloned.1.call-done = bf16[3,96,192]{1,2,0:T(8,128)(2,1)} async-done(((bf16[3,96,768]{1,2,0:T(8,128)(2,1)}), bf16[3,96,192]{1,2,0:T(8,128)(2,1)}) %reduce-scatter.27.cloned.1.call-update) | async-done | bytes 110608 | tf_op jit(solution)/shard_map/reduce_scatter | solution.py:159
  961.5 23.2 %reduce-scatter.25.cloned.1.call-done = bf16[3,96,192]{1,2,0:T(8,128)(2,1)} async-done(((bf16[3,96,768]{1,2,0:T(8,128)(2,1)}), bf16[3,96,192]{1,2,0:T(8,128)(2,1)}) %reduce-scatter.25.cloned.1.call-update) | async-done | bytes 110608 | tf_op jit(solution)/shard_map/reduce_scatter | solution.py:159
  986.9 20.5 %reduce-scatter.39.cloned.1.call-done = bf16[96,768]{1,0:T(8,128)(2,1)} async-done(((bf16[96,3072]{1,0:T(8,128)(2,1)}), bf16[96,768]{1,0:T(8,128)(2,1)}) %reduce-scatter.39.cloned.1.call-update) | async-done | bytes 147472 | tf_op jit(solution)/shard_map/reduce_scatter | solution.py:159
  1007.4 22.7 %reduce-scatter.35.cloned.1.call-done = bf16[96,768]{1,0:T(8,128)(2,1)} async-done(((bf16[96,3072]{1,0:T(8,128)(2,1)}), bf16[96,768]{1,0:T(8,128)(2,1)}) %reduce-scatter.35.cloned.1.call-update) | async-done | bytes 147472 | tf_op jit(solution)/shard_map/reduce_scatter | solution.py:159
  1030.1 1.8 maximum_convert_fusion.1
  1032.0 20.7 %reduce-scatter.47.cloned.1.call-done = bf16[768,96]{0,1:T(8,128)(2,1)} async-done(((bf16[3072,96]{0,1:T(8,128)(2,1)}), bf16[768,96]{0,1:T(8,128)(2,1)}) %reduce-scatter.47.cloned.1.call-update) | async-done | bytes 147472 | tf_op jit(solution)/shard_map/reduce_scatter | solution.py:159
  1052.7 22.7 %reduce-scatter.43.cloned.1.call-done = bf16[768,96]{0,1:T(8,128)(2,1)} async-done(((bf16[3072,96]{0,1:T(8,128)(2,1)}), bf16[768,96]{0,1:T(8,128)(2,1)}) %reduce-scatter.43.cloned.1.call-update) | async-done | bytes 147472 | tf_op jit(solution)/shard_map/reduce_scatter | solution.py:159
  (290 shorter events, 59.2 us)
Async XLA Ops:
  7.2 204.0 %all-gather.26.cloned.1.call-start = ((), (), s32[]{:S(2)}) async-start(), calls=%async_computation.32 | async-start | bytes 3981312 | tf_op jit(solution)/shard_map/all_gather | solution.py:154
  8.2 22.7 %copy-start.29 = (bf16[2,192,96]{2,1,0:T(8,128)(2,1)S(1)}, bf16[2,192,96]{2,1,0:T(8,128)(2,1)}, u32[]{:S(2)}) copy-start(bf16[2,192,96]{2,1,0:T(8,128)(2,1)} %param.18) | copy-start | bytes 221188
  29.7 17.5 %copy-start.27 = (bf16[2,96,768]{2,1,0:T(8,128)(2,1)S(1)}, bf16[2,96,768]{2,1,0:T(8,128)(2,1)}, u32[]{:S(2)}) copy-start(bf16[2,96,768]{2,1,0:T(8,128)(2,1)} %param.20) | copy-start | bytes 884740
  30.9 198.6 %all-gather.28.cloned.1.call-start = ((), (), s32[]{:S(2)}) async-start(), calls=%async_computation.33 | async-start | bytes 1327104 | tf_op jit(solution)/shard_map/all_gather | solution.py:154
  31.1 33.6 %copy-start.28 = (bf16[2,768,96]{1,2,0:T(8,128)(2,1)S(1)}, bf16[2,768,96]{1,2,0:T(8,128)(2,1)}, u32[]{:S(2)}) copy-start(bf16[2,768,96]{1,2,0:T(8,128)(2,1)} %param.22) | copy-start | bytes 884740
  47.2 186.0 %all-gather.30.cloned.1.call-start = ((), (), s32[]{:S(2)}) async-start(), calls=%async_computation.34 | async-start | bytes 5308416 | tf_op jit(solution)/shard_map/all_gather | solution.py:154
  64.6 176.8 %all-gather.32.cloned.1.call-start = ((), (), s32[]{:S(2)}) async-start(), calls=%async_computation.35 | async-start | bytes 5308416 | tf_op jit(solution)/shard_map/all_gather | solution.py:154
  80.5 171.5 %all-gather.34.cloned.1.call-start = ((), (), s32[]{:S(2)}) async-start(), calls=%async_computation.36 | async-start | bytes 3981312 | tf_op jit(solution)/shard_map/all_gather | solution.py:154
  98.6 34.3 %copy-start.25 = (bf16[128,3,768]{2,0,1:T(8,128)(2,1)S(1)}, bf16[128,3,768]{2,0,1:T(8,128)(2,1)}, u32[]{:S(2)}) copy-start(bf16[128,3,768]{2,0,1:T(8,128)(2,1)} %param.12) | copy-start | bytes 1769476
  98.6 171.5 %all-gather.36.cloned.1.call-start = ((), (), s32[]{:S(2)}) async-start(), calls=%async_computation.37 | async-start | bytes 1327104 | tf_op jit(solution)/shard_map/all_gather | solution.py:154
  114.7 162.5 %all-gather.38.cloned.1.call-start = ((), (), s32[]{:S(2)}) async-start(), calls=%async_computation.38 | async-start | bytes 5308416 | tf_op jit(solution)/shard_map/all_gather | solution.py:154
  133.8 27.8 %copy-start.32 = (bf16[2,2,24]{2,1,0:T(2,128)(2,1)S(1)}, bf16[2,2,24]{2,1,0:T(2,128)(2,1)}, u32[]{:S(2)}) copy-start(bf16[2,2,24]{2,1,0:T(2,128)(2,1)} %param.14) | copy-start | bytes 580
  133.8 27.9 %copy-start.33 = (bf16[2,2,24]{2,1,0:T(2,128)(2,1)S(1)}, bf16[2,2,24]{2,1,0:T(2,128)(2,1)}, u32[]{:S(2)}) copy-start(bf16[2,2,24]{2,1,0:T(2,128)(2,1)} %param.15) | copy-start | bytes 580
  133.8 28.0 %copy-start.34 = (bf16[2,2,24]{2,1,0:T(2,128)(2,1)S(1)}, bf16[2,2,24]{2,1,0:T(2,128)(2,1)}, u32[]{:S(2)}) copy-start(bf16[2,2,24]{2,1,0:T(2,128)(2,1)} %param.17) | copy-start | bytes 580
  133.8 28.1 %copy-start.35 = (bf16[2,24]{1,0:T(2,128)(2,1)S(1)}, bf16[2,24]{1,0:T(2,128)(2,1)}, u32[]{:S(2)}) copy-start(bf16[2,24]{1,0:T(2,128)(2,1)} %param.19) | copy-start | bytes 292
  133.8 28.1 %copy-start.36 = (bf16[2,96]{1,0:T(2,128)(2,1)S(1)}, bf16[2,96]{1,0:T(2,128)(2,1)}, u32[]{:S(2)}) copy-start(bf16[2,96]{1,0:T(2,128)(2,1)} %param.21) | copy-start | bytes 1156
  133.9 28.2 %copy-start.37 = (bf16[2,24]{1,0:T(2,128)(2,1)S(1)}, bf16[2,24]{1,0:T(2,128)(2,1)}, u32[]{:S(2)}) copy-start(bf16[2,24]{1,0:T(2,128)(2,1)} %param.23) | copy-start | bytes 292
  133.9 72.8 %all-to-all-start = ((bf16[4,128,768]{2,1,0:T(8,128)(2,1)}), bf16[4,128,768]{2,1,0:T(8,128)(2,1)S(1)}, u32[]{:S(2)}, u32[]{:S(2)}) async-start(bf16[4,128,768]{2,1,0:T(8,128)(2,1)} %pad.7), calls=%async_computation | async-start | bytes 1572864 | tf_op jit(solution)/shard_map/all_to_all | solution.py:141
  139.8 178.2 %all-gather.40.cloned.1.call-start = ((), (), s32[]{:S(2)}) async-start(), calls=%async_computation.39 | async-start | bytes 5308416 | tf_op jit(solution)/shard_map/all_gather | solution.py:154
  139.8 65.7 %copy-start.26 = (bf16[128,3,768]{2,0,1:T(8,128)(2,1)S(1)}, bf16[128,3,768]{2,0,1:T(8,128)(2,1)}, u32[]{:S(2)}) copy-start(bf16[128,3,768]{2,0,1:T(8,128)(2,1)} %param.13) | copy-start | bytes 1769476
  206.7 22.8 %copy-start.6 = (bf16[4,128,768]{2,1,0:T(8,128)(2,1)}, bf16[4,128,768]{2,1,0:T(8,128)(2,1)S(1)}, u32[]{:S(2)}) copy-start(bf16[4,128,768]{2,1,0:T(8,128)(2,1)S(1)} %all-to-all-done) | copy-start | bytes 2359300
  206.7 78.7 %all-to-all-start.2 = ((bf16[4,128,768]{2,1,0:T(8,128)(2,1)}), bf16[4,128,768]{2,1,0:T(8,128)(2,1)S(1)}, u32[]{:S(2)}, u32[]{:S(2)}) async-start(bf16[4,128,768]{2,1,0:T(8,128)(2,1)} %pad.8), calls=%async_computation.2 | async-start | bytes 1572864 | tf_op jit(solution)/shard_map/all_to_all | solution.py:141
  210.2 274.5 %reduce-scatter.31.cloned.1.call-start = ((), (), s32[]{:S(2)}) async-start(), calls=%async_computation.23 | async-start | bytes 1327104 | tf_op jit(solution)/shard_map/reduce_scatter | solution.py:158
  268.7 1.4 copy-start.2
  285.4 42.3 %copy-start.9 = (bf16[4,128,768]{2,1,0:T(8,128)(2,1)}, bf16[4,128,768]{2,1,0:T(8,128)(2,1)S(1)}, u32[]{:S(2)}) copy-start(bf16[4,128,768]{2,1,0:T(8,128)(2,1)S(1)} %all-to-all-done.2) | copy-start | bytes 2359300
  318.0 9.7 copy-start.13
  318.0 9.7 copy-start.30
  327.7 3.1 copy-start.38
  327.7 3.1 copy-start.10
  331.5 1.9 copy-start.8
  333.4 2.2 copy-start.3
  335.6 19.6 %copy-start.20 = (f32[512,768]{1,0:T(8,128)S(1)}, f32[512,768]{1,0:T(8,128)}, u32[]{:S(2)}) copy-start(f32[512,768]{1,0:T(8,128)} %copy-done.19) | copy-start | bytes 4718596
  335.6 19.6 %copy-start.31 = (bf16[1,3,768,768]{3,2,1,0:T(8,128)(2,1)S(1)}, bf16[1,3,768,768]{3,2,1,0:T(8,128)(2,1)}, u32[]{:S(2)}) copy-start(bf16[1,3,768,768]{3,2,1,0:T(8,128)(2,1)} %all-gather.34.cloned.1.call-done) | copy-start | bytes 10616836
  358.6 128.0 %reduce-scatter.29.cloned.1.call-start = ((), (), s32[]{:S(2)}) async-start(), calls=%async_computation.22 | async-start | bytes 1327104 | tf_op jit(solution)/shard_map/reduce_scatter | solution.py:158
  358.6 13.5 %slice-start = ((s8[4718592]{0:T(1024)(128)(4,1)}), s8[4194304]{0:T(1024)(128)(4,1)S(1)}, s32[]{:S(2)}) async-start(s8[4718592]{0:T(1024)(128)(4,1)} %bitcast.257), calls=%async_computation.45 | async-start | bytes 8388608
  361.7 13.5 %copy-start.21 = (f32[512,768]{1,0:T(8,128)}, f32[512,768]{1,0:T(8,128)S(1)}, u32[]{:S(2)}) copy-start(f32[512,768]{1,0:T(8,128)S(1)} %get-tuple-element.110) | copy-start | bytes 4718596
  361.7 10.4 copy-start.17
  361.7 10.4 slice-start.1
  372.1 3.1 copy-start.39
  380.3 108.3 %reduce-scatter.51.cloned.1.call-start = ((), (), s32[]{:S(2)}) async-start(), calls=%async_computation.41 | async-start | bytes 3981312
  399.0 2.7 copy-start.1
  399.0 139.8 %reduce-scatter.49.cloned.1.call-start = ((), (), s32[]{:S(2)}) async-start(), calls=%async_computation.40 | async-start | bytes 3981312
  401.7 20.5 %copy-start.24 = (bf16[512,768]{1,0:T(8,128)(2,1)S(1)}, bf16[512,768]{1,0:T(8,128)(2,1)}, u32[]{:S(2)}) copy-start(bf16[512,768]{1,0:T(8,128)(2,1)} %copy-done.23) | copy-start | bytes 2359300
  439.1 1.4 copy-start.14
  439.2 157.0 %reduce-scatter.37.cloned.1.call-start = ((), (), s32[]{:S(2)}) async-start(), calls=%async_computation.26 | async-start | bytes 5308416 | tf_op jit(solution)/shard_map/reduce_scatter | solution.py:158
  447.1 1.6 copy-start.18
  447.1 206.7 %reduce-scatter.33.cloned.1.call-start = ((), (), s32[]{:S(2)}) async-start(), calls=%async_computation.24 | async-start | bytes 5308416 | tf_op jit(solution)/shard_map/reduce_scatter | solution.py:158
  455.3 255.6 %reduce-scatter.45.cloned.1.call-start = ((), (), s32[]{:S(2)}) async-start(), calls=%async_computation.30 | async-start | bytes 5308416 | tf_op jit(solution)/shard_map/reduce_scatter | solution.py:158
  464.6 1.4 copy-start.22
  464.6 303.9 %reduce-scatter.41.cloned.1.call-start = ((), (), s32[]{:S(2)}) async-start(), calls=%async_computation.28 | async-start | bytes 5308416 | tf_op jit(solution)/shard_map/reduce_scatter | solution.py:158
  474.2 1.9 copy-start.5
  474.2 2.1 copy-start.7
  474.2 419.8 %all-reduce.6.cloned.1.call-start = ((), (), s32[]{:S(2)}) async-start(), calls=%async_computation.44 | async-start | bytes 163840
  484.6 433.4 %reduce-scatter.55.cloned.1.call-start = ((), (), s32[]{:S(2)}) async-start(), calls=%async_computation.43 | async-start | bytes 245760
  486.5 452.1 %reduce-scatter.53.cloned.1.call-start = ((), (), s32[]{:S(2)}) async-start(), calls=%async_computation.42 | async-start | bytes 245760
  488.3 473.2 %reduce-scatter.27.cloned.1.call-start = ((), (), s32[]{:S(2)}) async-start(), calls=%async_computation.21 | async-start | bytes 737280 | tf_op jit(solution)/shard_map/reduce_scatter | solution.py:159
  491.5 493.3 %reduce-scatter.25.cloned.1.call-start = ((), (), s32[]{:S(2)}) async-start(), calls=%async_computation.20 | async-start | bytes 737280 | tf_op jit(solution)/shard_map/reduce_scatter | solution.py:159
  540.4 113.4 %copy-start.15 = (f32[512,768]{1,0:T(8,128)S(1)}, f32[512,768]{1,0:T(8,128)}, u32[]{:S(2)}) copy-start(f32[512,768]{1,0:T(8,128)} %copy-done.12) | copy-start | bytes 4718596
  541.6 465.8 %reduce-scatter.39.cloned.1.call-start = ((), (), s32[]{:S(2)}) async-start(), calls=%async_computation.27 | async-start | bytes 737280 | tf_op jit(solution)/shard_map/reduce_scatter | solution.py:159
  596.2 434.0 %reduce-scatter.35.cloned.1.call-start = ((), (), s32[]{:S(2)}) async-start(), calls=%async_computation.25 | async-start | bytes 737280 | tf_op jit(solution)/shard_map/reduce_scatter | solution.py:159
  662.9 51.4 %all-to-all-start.1 = ((bf16[4,128,768]{2,1,0:T(8,128)(2,1)}), bf16[4,128,768]{2,1,0:T(8,128)(2,1)S(1)}, u32[]{:S(2)}, u32[]{:S(2)}) async-start(bf16[4,128,768]{2,1,0:T(8,128)(2,1)} %bitcast.30), calls=%async_computation.1 | async-start | bytes 1572864 | tf_op jit(solution)/shard_map/all_to_all | solution.py:148
  667.5 385.2 %reduce-scatter.47.cloned.1.call-start = ((), (), s32[]{:S(2)}) async-start(), calls=%async_computation.31 | async-start | bytes 737280 | tf_op jit(solution)/shard_map/reduce_scatter | solution.py:159
  714.3 186.9 %all-to-all-start.3 = ((bf16[4,128,768]{2,1,0:T(8,128)(2,1)}), bf16[4,128,768]{2,1,0:T(8,128)(2,1)S(1)}, u32[]{:S(2)}, u32[]{:S(2)}) async-start(bf16[4,128,768]{2,1,0:T(8,128)(2,1)} %bitcast.36), calls=%async_computation.3 | async-start | bytes 1572864 | tf_op jit(solution)/shard_map/all_to_all | solution.py:148
  718.9 356.4 %reduce-scatter.43.cloned.1.call-start = ((), (), s32[]{:S(2)}) async-start(), calls=%async_computation.29 | async-start | bytes 737280 | tf_op jit(solution)/shard_map/reduce_scatter | solution.py:159
  (7 other events, 8.2 us)
Sparse Core Ops, SparseCore 0:
  31.0 33.3 all-gather.25
  66.8 24.0 all-gather.27
  92.8 38.9 all-gather.29
  133.5 39.4 all-gather.31
  175.4 34.5 all-gather.33
  212.3 23.9 all-gather.35
  238.2 38.9 all-gather.37
  279.0 38.9 all-gather.39
  358.7 36.7 reduce-scatter.30
  398.9 36.7 reduce-scatter.28
  439.2 48.0 reduce-scatter.50
  490.7 48.0 reduce-scatter.48
  542.2 53.8 reduce-scatter.36
  599.8 53.8 reduce-scatter.32
  657.1 53.8 reduce-scatter.44
  714.6 53.8 reduce-scatter.40
  774.6 119.4 all-reduce.5
  896.7 21.2 reduce-scatter.54
  921.0 17.5 reduce-scatter.52
  941.3 20.2 reduce-scatter.26
  964.4 20.3 reduce-scatter.24
  987.0 20.3 reduce-scatter.38
  1009.7 20.3 reduce-scatter.34
  1032.3 20.3 reduce-scatter.46
  1054.9 20.3 reduce-scatter.42

commit v2 on v1

--- a/solution.py
+++ b/solution.py
@@ -149,15 +149,90 @@
     return items[:sequences].transpose(1, 0, 2)
 
 
-def gather(weight, split, head):
-    weight = lax.all_gather(weight, "tensor", axis=head, tiled=True)
-    return lax.all_gather(weight, "dp", axis=split, tiled=True)
-
-
-def scatter(grad, split, head):
-    grad = lax.psum_scatter(grad.astype(BF16), "dp", scatter_dimension=split, tiled=True)
-    grad = lax.psum_scatter(grad, "tensor", scatter_dimension=head, tiled=True)
+def bits_of(axis):
+    return [1 << bit for bit in range((lax.axis_size(axis) - 1).bit_length())]
+
+
+def partner(axis, mask):
+    return [(index, index ^ mask) for index in range(lax.axis_size(axis))]
+
+
+def own_bit(axis, mask):
+    return (lax.axis_index(axis) // mask) % 2
+
+
+def orders(turned):
+    masks = bits_of("dp")
+    outer = masks[1:][::-1] if turned else masks[1:]
+    return outer + masks[:1]
+
+
+def join_step(array, axis, mask, place):
+    other = lax.ppermute(array, axis, partner(axis, mask))
+    low = own_bit(axis, mask) == 0
+    first, second = jnp.where(low, array, other), jnp.where(low, other, array)
+    return jnp.stack([first, second], axis=place)
+
+
+def halve_step(array, axis, mask, place):
+    bit = own_bit(axis, mask)
+    kept = lax.dynamic_index_in_dim(array, bit, place, keepdims=False)
+    sent = lax.dynamic_index_in_dim(array, 1 - bit, place, keepdims=False)
+    arrived = lax.ppermute(sent, axis, partner(axis, mask))
+    return (kept.astype(F32) + arrived.astype(F32)).astype(array.dtype)
+
+
+def gather(weight, turned):
+    lead = weight.ndim - 2
+    for mask in bits_of("tensor"):
+        weight = join_step(weight, "tensor", mask, 0)
+    parts = lax.axis_size("tensor")
+    weight = weight.reshape((parts,) + weight.shape[-2 - lead :])
+    weight = jnp.moveaxis(weight, 0, -2)
+    weight = weight.reshape(weight.shape[:-2] + (-1,))
+    held = []
+    for mask in orders(turned):
+        place = sum(1 for other in held if other > mask)
+        held.append(mask)
+        weight = join_step(weight, "dp", mask, lead + place)
+    return weight.reshape(weight.shape[:lead] + (-1, weight.shape[-1]))
+
+
+def scatter(grad, turned):
+    lead = grad.ndim - 2
+    grad = grad.astype(BF16)
+    masks = bits_of("dp")
+    rows = grad.shape[lead] >> len(masks)
+    grad = grad.reshape(grad.shape[:lead] + (2,) * len(masks) + (rows, grad.shape[-1]))
+    held = masks
+    for mask in orders(turned)[::-1]:
+        place = sum(1 for other in held if other > mask)
+        held = [other for other in held if other != mask]
+        grad = halve_step(grad, "dp", mask, lead + place)
+    parts = lax.axis_size("tensor")
+    grad = grad.reshape(grad.shape[:-1] + (parts, -1))
+    grad = jnp.moveaxis(grad, -2, 0)
+    grad = grad.reshape((2,) * len(bits_of("tensor")) + grad.shape[1:])
+    for mask in bits_of("tensor")[::-1]:
+        grad = halve_step(grad, "tensor", mask, 0)
     return grad.astype(F32)
+
+
+def gather_small(packed):
+    packed = packed[None]
+    for axis in ("tensor", "dp"):
+        for mask in bits_of(axis):
+            packed = join_step(packed, axis, mask, 0)
+            packed = packed.reshape((-1,) + packed.shape[2:])
+    return packed
+
+
+def scatter_small(packed):
+    for axis in ("dp", "tensor"):
+        for mask in bits_of(axis)[::-1]:
+            packed = packed.reshape((2, -1) + packed.shape[1:])
+            packed = halve_step(packed, axis, mask, 0)
+    return packed[0]
 
 
 def on_device(
@@ -176,10 +251,9 @@
 ):
     sequences = inputs.shape[1]
     layers = attention_weight.shape[0]
-    both = ("dp", "tensor")
     small = (norm_gain, norm_shift, attention_bias, output_bias, expand_bias, contract_bias)
     packed = jnp.concatenate([item.reshape(-1) for item in small])
-    packed = lax.all_gather(packed, both, axis=0, tiled=False).astype(F32)
+    packed = gather_small(packed).astype(F32)
     shared = []
     start = 0
     for item in small:
@@ -191,10 +265,10 @@
     for layer in range(layers):
         weights.append(
             (
-                gather(attention_weight[layer], 1, 2),
-                gather(output_weight[layer], 1, 0),
-                gather(expand_weight[layer], 0, 1),
-                gather(contract_weight[layer], 1, 0),
+                gather(attention_weight[layer], layer % 2 == 1),
+                gather(output_weight[layer].T, layer % 2 == 0),
+                gather(expand_weight[layer], False),
+                gather(contract_weight[layer].T, True),
             )
         )
     residual = to_sequences(inputs).astype(F32)
@@ -210,13 +284,13 @@
         qkv = jnp.einsum("ld,cde->cle", normed, attention, preferred_element_type=F32)
         qkv = (qkv + shift[:, None]).astype(BF16)
         context = attend(qkv)
-        middle = residual + dot(context, output, ((1,), (0,))) + output_shift[layer]
+        middle = residual + dot(context, output, ((1,), (1,))) + output_shift[layer]
         scaled, inverse = norm_stats(middle)
         expanded = (scaled * gains[layer, 1] + shifts[layer, 1]).astype(BF16)
         hidden = dot(expanded, expand, ((1,), (0,))) + expand_shift[layer]
         active = smooth_unit(hidden).astype(BF16)
         stored.append((residual, normed, qkv, context, middle, expanded, hidden, active))
-        residual = middle + dot(active, contract, ((1,), (0,))) + contract_shift[layer]
+        residual = middle + dot(active, contract, ((1,), (1,))) + contract_shift[layer]
     outputs = to_positions(residual.astype(BF16), sequences)
     upstream = to_sequences(cotangent).astype(F32)
     weight_parts = []
@@ -226,13 +300,13 @@
         before, normed, qkv, context, middle, expanded, hidden, active = stored[layer]
         contract_bias_grad = jnp.sum(upstream, axis=0)
         upstream_low = upstream.astype(BF16)
-        contract_grad = scatter(dot(active, upstream_low, ((0,), (0,))), 1, 0)
-        grad_active = dot(upstream_low, contract, ((1,), (1,)))
+        contract_grad = scatter(dot(upstream_low, active, ((0,), (0,))), True).T
+        grad_active = dot(upstream_low, contract, ((1,), (0,)))
         unused, pull_unit = jax.vjp(smooth_unit, hidden)
         grad_hidden = pull_unit(grad_active)[0]
         expand_bias_grad = jnp.sum(grad_hidden, axis=0)
         hidden_low = grad_hidden.astype(BF16)
-        expand_grad = scatter(dot(expanded, hidden_low, ((0,), (0,))), 0, 1)
+        expand_grad = scatter(dot(expanded, hidden_low, ((0,), (0,))), False)
         grad_second = dot(hidden_low, expand, ((1,), (1,)))
         scaled, inverse = norm_stats(middle)
         second_gain = jnp.sum(grad_second * scaled, axis=0)
@@ -240,11 +314,11 @@
         grad_middle = upstream + norm_back(grad_second, gains[layer, 1], scaled, inverse)
         output_bias_grad = jnp.sum(grad_middle, axis=0)
         middle_low = grad_middle.astype(BF16)
-        output_grad = scatter(dot(context, middle_low, ((0,), (0,))), 1, 0)
-        grad_context = dot(middle_low, output, ((1,), (1,))).astype(BF16)
+        output_grad = scatter(dot(middle_low, context, ((0,), (0,))), layer % 2 == 0).T
+        grad_context = dot(middle_low, output, ((1,), (0,))).astype(BF16)
         grad_qkv, attention_bias_grad = attend_back(qkv, grad_context)
         attention_grad = scatter(
-            jnp.einsum("ld,cle->cde", normed, grad_qkv, preferred_element_type=F32), 1, 2
+            jnp.einsum("ld,cle->cde", normed, grad_qkv, preferred_element_type=F32), layer % 2 == 1
         )
         grad_first = jnp.einsum("cle,cde->ld", grad_qkv, attention, preferred_element_type=F32)
         scaled, inverse = norm_stats(before)
@@ -270,7 +344,7 @@
         grad = grad.reshape(item.shape[:-1] + (-1, item.shape[-1]))
         pieces.append(jnp.moveaxis(grad, -2, 0).reshape(-1, item.size))
     packed = jnp.concatenate(pieces, axis=1)
-    packed = lax.psum_scatter(packed, both, scatter_dimension=0, tiled=True)[0]
+    packed = scatter_small(packed)
     small_out = []
     start = 0
     for item in small:

time: 1090 us -> 761 us (0.70)
  waiting for transfers between devices: 580 us -> 313 us
  blocking collectives: 182 us -> 0 us
  starting transfers between devices: 20.2 us -> 105 us
  other arithmetic: 18.1 us -> 94.1 us
  matrix products: 132 us -> 91.4 us
  between operations: 15.6 us -> 3.9 us
    reduce_scatter x12 -> x0, waiting for transfers between devices: 336 us -> none  [the longest x6 205 us: scatter(): lax.psum_scatter(grad.astype(BF16), 'dp', scatter_dimension=split, tiled=...]
    ppermute x0 -> x90, waiting for transfers between devices: none -> 306 us  [the longest x45 195 us: halve_step(): arrived = lax.ppermute(sent, axis, partner(axis, mask))]
    unnamed x30 -> x0, waiting for transfers between devices: 208 us -> none
    all_gather x8 -> x0, blocking collectives: 141 us -> none  [gather(): weight = lax.all_gather(weight, 'tensor', axis=head, tiled=True)]
    ppermute x0 -> x90, starting transfers between devices: none -> 88.6 us  [the longest x45 50.3 us: join_step(): other = lax.ppermute(array, axis, partner(axis, mask))]
    another operation x0 -> x82, other arithmetic: none -> 50 us  [join_step(): return jnp.stack([first, second], axis=place)]
    unnamed x1 -> x0, blocking collectives: 41 us -> none
    unnamed x104 -> x237, local copies, waits for them, and re-layouts: 53.3 us -> 12.3 us
  transfers between devices with their start and end apart: 29 -> 94, of which waited for: 16 -> 41; matrix products, arithmetic and copies ran while one was open for 17% -> 23% of each run, Pallas kernels for 4% -> 6%
where the time goes in v2:
time: 761 us; the launch traced here: 750 us
  waiting for transfers between devices  313 us (41%)
  starting transfers between devices  105 us (14%)
  other arithmetic  94.1 us (12%)
  matrix products  91.4 us (12%)
  local copies, waits for them, and re-layouts  79 us (10%)
  Pallas kernels  62.9 us (8%)
    ppermute x45, waiting for transfers between devices, halve_step(): arrived = lax.ppermute(sent, axis, partner(axis, mask))  195 us
    ppermute x45, waiting for transfers between devices, join_step(): other = lax.ppermute(array, axis, partner(axis, mask))  111 us
    dot_general x18, matrix products, dot(): lax.dot_general(left, right, (contract, ((), ())), preferred_element_type...  72.8 us
    ppermute x45, starting transfers between devices, join_step(): other = lax.ppermute(array, axis, partner(axis, mask))  50.3 us
    another operation x82, other arithmetic, join_step(): return jnp.stack([first, second], axis=place)  50 us
    pallas_call x2, Pallas kernels, attend_back(): pl.pallas_call(attend_back_kernel, grid=(width // 128,), in_specs=[pl.Blo...  38.7 us
    ppermute x45, starting transfers between devices, halve_step(): arrived = lax.ppermute(sent, axis, partner(axis, mask))  38.3 us
    convert_element_type x32, other arithmetic, halve_step(): return (kept.astype(F32) + arrived.astype(F32)).astype(array.dtype)  28.9 us
  transfers between devices with their start and end apart: 94, of which 41 were waited for; matrix products, arithmetic and copies ran while one was open for 23% of the time, Pallas kernels for 6%

profile of v2, /device:TPU:0, one launch (start us, length us, event | category | flops | bytes accessed | tf_op | source)
XLA Modules:
  0.0 749.9 jit_solution(17050510570640939758)
XLA Ops:
  5.3 3.1 collective-permute-start.5
  10.4 4.0 all-to-all-start
  14.5 3.0 collective-permute-start.6
  20.2 14.3 %collective-permute-done.6 = bf16[2,576]{1,0:T(2,128)(2,1)S(1)} collective-permute-done((bf16[2,576]{1,0:T(2,128)(2,1)S(1)}, bf16[2,576]{1,0:T(2,128)(2,1)S(1)}, u32[]{:S(2)}, u32[]{:S(2)}) %collective-permute-start.6) | collective-permute-done | bytes 2336 | tf_op jit(solution)/shard_map/ppermute | solution.py:171
  57.4 5.2 collective-permute-done.31
  64.8 3.4 collective-permute-start.26
  79.5 2.9 collective-permute-start.41
  84.0 23.4 %collective-permute-done.26 = bf16[2,3,96,192]{3,2,1,0:T(8,128)(2,1)} collective-permute-done((bf16[2,3,96,192]{3,2,1,0:T(8,128)(2,1)}, bf16[2,3,96,192]{3,2,1,0:T(8,128)(2,1)}, u32[]{:S(2)}, u32[]{:S(2)}) %collective-permute-start.26) | collective-permute-done | bytes 221216 | tf_op jit(solution)/shard_map/ppermute | solution.py:171
  107.4 9.4 %collective-permute-done.1 = bf16[2,3,96,192]{3,2,1,0:T(8,128)(2,1)S(1)} collective-permute-done((bf16[2,3,96,192]{3,2,1,0:T(8,128)(2,1)S(1)}, bf16[2,3,96,192]{3,2,1,0:T(8,128)(2,1)S(1)}, u32[]{:S(2)}, u32[]{:S(2)}) %collective-permute-start.1) | collective-permute-done | bytes 221216 | tf_op jit(solution)/shard_map/ppermute | solution.py:171
  126.2 3.3 collective-permute-done.16
  132.6 3.2 collective-permute-done.41
  151.0 9.5 %collective-permute-done.22 = bf16[96,3072]{1,0:T(8,128)(2,1)S(1)} collective-permute-done((bf16[96,3072]{1,0:T(8,128)(2,1)S(1)}, bf16[96,3072]{1,0:T(8,128)(2,1)S(1)}, u32[]{:S(2)}, u32[]{:S(2)}) %collective-permute-start.22) | collective-permute-done | bytes 589856 | tf_op jit(solution)/shard_map/ppermute | solution.py:171
  163.4 9.8 %collective-permute-done.42 = bf16[96,3072]{1,0:T(8,128)(2,1)S(1)} collective-permute-done((bf16[96,3072]{1,0:T(8,128)(2,1)S(1)}, bf16[96,3072]{1,0:T(8,128)(2,1)S(1)}, u32[]{:S(2)}, u32[]{:S(2)}) %collective-permute-start.42) | collective-permute-done | bytes 589856 | tf_op jit(solution)/shard_map/ppermute | solution.py:171
  181.7 4.2 all-to-all-start.2
  191.6 7.4 all-to-all-done.2
  206.8 14.6 %collective-permute-done.23 = bf16[2,96,3072]{2,1,0:T(8,128)(2,1)} collective-permute-done((bf16[2,96,3072]{2,1,0:T(8,128)(2,1)}, bf16[2,96,3072]{2,1,0:T(8,128)(2,1)}, u32[]{:S(2)}, u32[]{:S(2)}) %collective-permute-start.23) | collective-permute-done | bytes 1179680 | tf_op jit(solution)/shard_map/ppermute | solution.py:171
  225.8 13.8 %collective-permute-done.43 = bf16[2,96,3072]{2,1,0:T(8,128)(2,1)} collective-permute-done((bf16[2,96,3072]{2,1,0:T(8,128)(2,1)}, bf16[2,96,3072]{2,1,0:T(8,128)(2,1)}, u32[]{:S(2)}, u32[]{:S(2)}) %collective-permute-start.43) | collective-permute-done | bytes 1179680 | tf_op jit(solution)/shard_map/ppermute | solution.py:171
  252.1 12.3 %shard_map.211 = bf16[512,768]{1,0:T(8,128)(2,1)S(1)} custom-call(bf16[3,512,768]{2,1,0:T(8,128)(2,1)S(1)} %fusion.18.qkv_ref), custom_call_target="tpu_custom_call" | custom-call | flops 805306368 | bytes 3145728 | tf_op jit(solution)/shard_map/pallas_call | solution.py:94
  278.8 3.7 copy-done.29
  282.5 4.8 fusion.120
  287.3 6.3 fusion.133
  294.0 4.1 fusion.19.qkv_ref
  298.1 12.0 %shard_map.212 = bf16[512,768]{1,0:T(8,128)(2,1)S(1)} custom-call(bf16[3,512,768]{2,1,0:T(8,128)(2,1)S(1)} %fusion.19.qkv_ref), custom_call_target="tpu_custom_call" | custom-call | flops 805306368 | bytes 3145728 | tf_op jit(solution)/shard_map/pallas_call | solution.py:94
  317.8 6.6 fusion.123
  324.4 3.0 multiply_reduce_fusion
  329.5 19.3 %shard_map.213 = (bf16[3,512,768]{2,1,0:T(8,128)(2,1)S(1)}, f32[2,8,768]{2,1,0:T(8,128)S(1)}) custom-call(bf16[3,512,768]{2,1,0:T(8,128)(2,1)S(1)} %fusion.19.qkv_ref, bf16[512,768]{1,0:T(8,128)(2,1)S(1)} %convolution_convert_fusion.9.up_ref), custom_call_target="tpu_custom_call" | custom-call | flops 2013265920 | bytes 5505024 | tf_op jit(solution)/shard_map/pallas_call | solution.py:111
  351.2 4.1 convolution_convert_fusion.4
  357.8 9.1 %fusion.135 = (f32[3072]{0:T(1024)S(1)}, bf16[512,3072]{1,0:T(8,128)(2,1)S(1)}) fusion(f32[512,3072]{1,0:T(8,128)} %fusion.120, f32[3072]{0:T(1024)S(1)} %copy-done.76, bf16[768,3072]{1,0:T(8,128)(2,1)S(1)} %bitcast.791, f32[512,768]{1,0:T(8,128)S(1)} %get-tuple-element.50), kind=kOutput, calls=%fused_computation.473 | convolution fusion | flops 2450912256 | bytes 15753216 | tf_op jit(solution)/shard_map/dot_general | solution.py:36
  366.9 3.0 multiply_reduce_fusion.1
  374.1 4.8 convolution_convert_fusion.2
  378.9 4.8 convolution_convert_fusion.3
  383.7 8.1 %convolution_convert_fusion = bf16[768,3072]{1,0:T(8,128)(2,1)} fusion(bf16[512,768]{1,0:T(8,128)(2,1)S(1)} %bitcast.755, f32[512,3072]{1,0:T(8,128)} %copy-done.89, f32[3072]{0:T(1024)S(1)} %copy-done.77), kind=kOutput, calls=%fused_computation.18 | convolution fusion | flops 2434007040 | bytes 11808768 | tf_op jit(solution)/shard_map/dot_general | solution.py:36
  391.8 4.9 convolution_convert_fusion.1
  396.7 7.8 %add_convert_fusion.2 = bf16[512,768]{1,0:T(8,128)(2,1)} fusion(f32[512,768]{1,0:T(8,128)S(1)} %get-tuple-element.190, bf16[768,3072]{1,0:T(8,128)(2,1)S(1)} %bitcast.785, f32[768]{0:T(1024)S(1)} %copy-done.85, f32[512,3072]{1,0:T(8,128)} %copy-done.89, f32[3072]{0:T(1024)S(1)} %copy-done.77), kind=kOutput, calls=%fused_computation.127 | convolution fusion | flops 2432827392 | bytes 13384704 | tf_op jit(solution)/shard_map/dot_general | solution.py:36
  404.5 4.2 all-to-all-start.1
  408.8 19.3 %shard_map.214 = (bf16[3,512,768]{2,1,0:T(8,128)(2,1)S(1)}, f32[2,8,768]{2,1,0:T(8,128)S(1)}) custom-call(bf16[3,512,768]{2,1,0:T(8,128)(2,1)S(1)} %fusion.18.qkv_ref, bf16[512,768]{1,0:T(8,128)(2,1)S(1)} %convolution_convert_fusion.8.up_ref), custom_call_target="tpu_custom_call" | custom-call | flops 2013265920 | bytes 5505024 | tf_op jit(solution)/shard_map/pallas_call | solution.py:111
  428.2 4.0 fusion.26
  436.6 3.0 dynamic-slice_bitcast_fusion.4
  455.1 3.4 dynamic-slice_bitcast_fusion.2
  459.8 3.0 collective-permute-start.48
  477.5 6.9 collective-permute-done.66
  485.9 6.5 collective-permute-done.61
  494.0 3.5 collective-permute-done.67
  498.6 4.1 collective-permute-done.62
  505.4 5.8 collective-permute-done.68
  511.3 4.4 all-to-all-start.3
  515.8 5.3 collective-permute-done.63
  521.1 5.2 collective-permute-done.69
  527.3 4.7 collective-permute-done.64
  548.6 2.9 fusion.15
  554.0 2.9 fusion.12
  562.0 3.5 collective-permute-done.51
  568.4 55.9 %collective-permute-done.57 = bf16[3,96,768]{2,1,0:T(8,128)(2,1)S(1)} collective-permute-done((bf16[3,96,768]{2,1,0:T(8,128)(2,1)S(1)}, bf16[3,96,768]{2,1,0:T(8,128)(2,1)S(1)}, u32[]{:S(2)}, u32[]{:S(2)}) %collective-permute-start.57) | collective-permute-done | bytes 442400 | tf_op jit(solution)/shard_map/ppermute | solution.py:181
  635.9 8.8 %collective-permute-done.58 = bf16[2,3,96,192]{3,2,1,0:T(8,128)(2,1)} collective-permute-done((bf16[2,3,96,192]{3,2,1,0:T(8,128)(2,1)}, bf16[2,3,96,192]{3,2,1,0:T(8,128)(2,1)}, u32[]{:S(2)}, u32[]{:S(2)}) %collective-permute-start.58) | collective-permute-done | bytes 221216 | tf_op jit(solution)/shard_map/ppermute | solution.py:181
  645.9 14.4 %collective-permute-done.53 = bf16[2,3,96,192]{3,2,1,0:T(8,128)(2,1)S(1)} collective-permute-done((bf16[2,3,96,192]{3,2,1,0:T(8,128)(2,1)S(1)}, bf16[2,3,96,192]{3,2,1,0:T(8,128)(2,1)S(1)}, u32[]{:S(2)}, u32[]{:S(2)}) %collective-permute-start.53) | collective-permute-done | bytes 221216 | tf_op jit(solution)/shard_map/ppermute | solution.py:181
  660.3 5.7 collective-permute-done.59
  666.3 4.8 collective-permute-done.54
  683.7 6.6 collective-permute-done.77
  691.4 8.5 %collective-permute-done.72 = bf16[96,3072]{1,0:T(8,128)(2,1)S(1)} collective-permute-done((bf16[96,3072]{1,0:T(8,128)(2,1)S(1)}, bf16[96,3072]{1,0:T(8,128)(2,1)S(1)}, u32[]{:S(2)}, u32[]{:S(2)}) %collective-permute-start.72) | collective-permute-done | bytes 589856 | tf_op jit(solution)/shard_map/ppermute | solution.py:181
  708.1 19.1 %collective-permute-done.73 = bf16[2,96,768]{2,1,0:T(8,128)(2,1)S(1)} collective-permute-done((bf16[2,96,768]{2,1,0:T(8,128)(2,1)S(1)}, bf16[2,96,768]{2,1,0:T(8,128)(2,1)S(1)}, u32[]{:S(2)}, u32[]{:S(2)}) %collective-permute-start.73) | collective-permute-done | bytes 294944 | tf_op jit(solution)/shard_map/ppermute | solution.py:181
  727.4 6.2 collective-permute-done.88
  733.8 5.4 collective-permute-done.83
  739.5 2.9 collective-permute-done.74
  742.4 3.1 collective-permute-done.89
  (733 shorter events, 258.8 us)
Async XLA Ops:
  10.4 171.3 %all-to-all-start = ((bf16[4,128,768]{2,1,0:T(8,128)(2,1)}), bf16[4,128,768]{2,1,0:T(8,128)(2,1)S(1)}, u32[]{:S(2)}, u32[]{:S(2)}) async-start(bf16[4,128,768]{2,1,0:T(8,128)(2,1)} %pad.7), calls=%async_computation | async-start | bytes 1572864 | tf_op jit(solution)/shard_map/all_to_all | solution.py:141
  14.5 20.0 %collective-permute-start.6 = (bf16[2,576]{1,0:T(2,128)(2,1)S(1)}, bf16[2,576]{1,0:T(2,128)(2,1)S(1)}, u32[]{:S(2)}, u32[]{:S(2)}) collective-permute-start(bf16[2,576]{1,0:T(2,128)(2,1)S(1)} %bitcast.864), channel_id=1, source_target_pairs={{0,2},{1,3},{2,0},{3,1},{4,6},{5,7},{6,4},{7,5},{8,10},{9,11},{10,... | collective-permute-start | bytes 6920 | tf_op jit(solution)/shard_map/ppermute | solution.py:171
  18.1 35.4 %collective-permute-start.25 = (bf16[3,96,192]{2,1,0:T(8,128)(2,1)}, bf16[3,96,192]{2,1,0:T(8,128)(2,1)S(1)}, u32[]{:S(2)}, u32[]{:S(2)}) collective-permute-start(bf16[3,96,192]{2,1,0:T(8,128)(2,1)} %get-tuple-element.138), channel_id=1, source_target_pairs={{0,1},{1,0},{2,3},{3,2},{4,5},{5,4},{6,7},{7,6},{8,9},{9,8},{10,11... | collective-permute-start | bytes 331784 | tf_op jit(solution)/shard_map/ppermute | solution.py:171
  19.6 36.0 %collective-permute-start = (bf16[3,96,192]{2,1,0:T(8,128)(2,1)S(1)}, bf16[3,96,192]{2,1,0:T(8,128)(2,1)S(1)}, u32[]{:S(2)}, u32[]{:S(2)}) collective-permute-start(bf16[3,96,192]{2,1,0:T(8,128)(2,1)S(1)} %get-tuple-element.139), channel_id=1, source_target_pairs={{0,1},{1,0},{2,3},{3,2},{4,5},{5,4},{6,7},{7,6},{8,9},{9,8},{10,11... | collective-permute-start | bytes 331784 | tf_op jit(solution)/shard_map/ppermute | solution.py:171
  34.6 16.8 %collective-permute-start.30 = (bf16[96,192]{0,1:T(8,128)(2,1)S(1)}, bf16[96,192]{0,1:T(8,128)(2,1)S(1)}, u32[]{:S(2)}, u32[]{:S(2)}) collective-permute-start(bf16[96,192]{0,1:T(8,128)(2,1)S(1)} %get-tuple-element.152), channel_id=1, source_target_pairs={{0,1},{1,0},{2,3},{3,2},{4,5},{5,4},{6,7},{7,6},{8,9},{9,8},{10,11... | collective-permute-start | bytes 110600 | tf_op jit(solution)/shard_map/ppermute | solution.py:171
  34.7 18.7 %collective-permute-start.10 = (bf16[96,192]{0,1:T(8,128)(2,1)S(1)}, bf16[96,192]{0,1:T(8,128)(2,1)S(1)}, u32[]{:S(2)}, u32[]{:S(2)}) collective-permute-start(bf16[96,192]{0,1:T(8,128)(2,1)S(1)} %get-tuple-element.153), channel_id=1, source_target_pairs={{0,1},{1,0},{2,3},{3,2},{4,5},{5,4},{6,7},{7,6},{8,9},{9,8},{10,11... | collective-permute-start | bytes 110600 | tf_op jit(solution)/shard_map/ppermute | solution.py:171
  44.4 24.8 %collective-permute-start.40 = (bf16[96,768]{1,0:T(8,128)(2,1)}, bf16[96,768]{1,0:T(8,128)(2,1)S(1)}, u32[]{:S(2)}, u32[]{:S(2)}) collective-permute-start(bf16[96,768]{1,0:T(8,128)(2,1)} %get-tuple-element.132), channel_id=1, source_target_pairs={{0,1},{1,0},{2,3},{3,2},{4,5},{5,4},{6,7},{7,6},{8,9},{9,8},{10,11... | collective-permute-start | bytes 442376 | tf_op jit(solution)/shard_map/ppermute | solution.py:171
  51.5 17.8 %collective-permute-start.20 = (bf16[96,768]{1,0:T(8,128)(2,1)}, bf16[96,768]{1,0:T(8,128)(2,1)S(1)}, u32[]{:S(2)}, u32[]{:S(2)}) collective-permute-start(bf16[96,768]{1,0:T(8,128)(2,1)} %get-tuple-element.133), channel_id=1, source_target_pairs={{0,1},{1,0},{2,3},{3,2},{4,5},{5,4},{6,7},{7,6},{8,9},{9,8},{10,11... | collective-permute-start | bytes 442376 | tf_op jit(solution)/shard_map/ppermute | solution.py:171
  53.4 17.5 %collective-permute-start.15 = (bf16[96,768]{1,0:T(8,128)(2,1)}, bf16[96,768]{1,0:T(8,128)(2,1)S(1)}, u32[]{:S(2)}, u32[]{:S(2)}) collective-permute-start(bf16[96,768]{1,0:T(8,128)(2,1)} %get-tuple-element.129), channel_id=1, source_target_pairs={{0,1},{1,0},{2,3},{3,2},{4,5},{5,4},{6,7},{7,6},{8,9},{9,8},{10,11... | collective-permute-start | bytes 442376 | tf_op jit(solution)/shard_map/ppermute | solution.py:171
  64.8 42.7 %collective-permute-start.26 = (bf16[2,3,96,192]{3,2,1,0:T(8,128)(2,1)}, bf16[2,3,96,192]{3,2,1,0:T(8,128)(2,1)}, u32[]{:S(2)}, u32[]{:S(2)}) collective-permute-start(bf16[2,3,96,192]{3,2,1,0:T(8,128)(2,1)} %pad_maximum_fusion.32), channel_id=1, source_target_pairs={{0,2},{1,3},{2,0},{3,1},{4,6},{5,7},{6,4},{7,5},{8,10},{9,11},{10,... | collective-permute-start | bytes 663560 | tf_op jit(solution)/shard_map/ppermute | solution.py:171
  69.2 47.6 %collective-permute-start.1 = (bf16[2,3,96,192]{3,2,1,0:T(8,128)(2,1)S(1)}, bf16[2,3,96,192]{3,2,1,0:T(8,128)(2,1)S(1)}, u32[]{:S(2)}, u32[]{:S(2)}) collective-permute-start(bf16[2,3,96,192]{3,2,1,0:T(8,128)(2,1)S(1)} %pad_maximum_fusion.28), channel_id=1, source_target_pairs={{0,2},{1,3},{2,0},{3,1},{4,6},{5,7},{6,4},{7,5},{8,10},{9,11},{10,... | collective-permute-start | bytes 663560 | tf_op jit(solution)/shard_map/ppermute | solution.py:171
  74.3 49.1 %collective-permute-start.21 = (bf16[2,96,768]{2,1,0:T(8,128)(2,1)}, bf16[2,96,768]{2,1,0:T(8,128)(2,1)}, u32[]{:S(2)}, u32[]{:S(2)}) collective-permute-start(bf16[2,96,768]{2,1,0:T(8,128)(2,1)} %pad_maximum_fusion.31), channel_id=1, source_target_pairs={{0,2},{1,3},{2,0},{3,1},{4,6},{5,7},{6,4},{7,5},{8,10},{9,11},{10,... | collective-permute-start | bytes 884744 | tf_op jit(solution)/shard_map/ppermute | solution.py:171
  79.4 50.2 %collective-permute-start.16 = (bf16[2,96,768]{2,1,0:T(8,128)(2,1)}, bf16[2,96,768]{2,1,0:T(8,128)(2,1)}, u32[]{:S(2)}, u32[]{:S(2)}) collective-permute-start(bf16[2,96,768]{2,1,0:T(8,128)(2,1)} %pad_maximum_fusion.30), channel_id=1, source_target_pairs={{0,2},{1,3},{2,0},{3,1},{4,6},{5,7},{6,4},{7,5},{8,10},{9,11},{10,... | collective-permute-start | bytes 884744 | tf_op jit(solution)/shard_map/ppermute | solution.py:171
  79.5 56.3 %collective-permute-start.41 = (bf16[2,96,768]{2,1,0:T(8,128)(2,1)}, bf16[2,96,768]{2,1,0:T(8,128)(2,1)}, u32[]{:S(2)}, u32[]{:S(2)}) collective-permute-start(bf16[2,96,768]{2,1,0:T(8,128)(2,1)} %pad_maximum_fusion.35), channel_id=1, source_target_pairs={{0,2},{1,3},{2,0},{3,1},{4,6},{5,7},{6,4},{7,5},{8,10},{9,11},{10,... | collective-permute-start | bytes 884744 | tf_op jit(solution)/shard_map/ppermute | solution.py:171
  107.4 33.2 %collective-permute-start.36 = (bf16[2,96,768]{2,1,0:T(8,128)(2,1)}, bf16[2,96,768]{2,1,0:T(8,128)(2,1)}, u32[]{:S(2)}, u32[]{:S(2)}) collective-permute-start(bf16[2,96,768]{2,1,0:T(8,128)(2,1)} %pad_maximum_fusion.34), channel_id=1, source_target_pairs={{0,2},{1,3},{2,0},{3,1},{4,6},{5,7},{6,4},{7,5},{8,10},{9,11},{10,... | collective-permute-start | bytes 884744 | tf_op jit(solution)/shard_map/ppermute | solution.py:171
  116.8 26.6 %collective-permute-start.13 = (bf16[2,96,768]{2,1,0:T(8,128)(2,1)}, bf16[2,96,768]{2,1,0:T(8,128)(2,1)}, u32[]{:S(2)}, u32[]{:S(2)}) collective-permute-start(bf16[2,96,768]{2,1,0:T(8,128)(2,1)} %pad_maximum_fusion.29), channel_id=1, source_target_pairs={{0,8},{4,12},{8,0},{12,4},{16,24},{20,28},{24,16},{28,20},{1,9},{5... | collective-permute-start | bytes 884744 | tf_op jit(solution)/shard_map/ppermute | solution.py:171
  123.4 23.5 %collective-permute-start.33 = (bf16[2,96,768]{2,1,0:T(8,128)(2,1)}, bf16[2,96,768]{2,1,0:T(8,128)(2,1)S(1)}, u32[]{:S(2)}, u32[]{:S(2)}) collective-permute-start(bf16[2,96,768]{2,1,0:T(8,128)(2,1)} %pad_maximum_fusion.33), channel_id=1, source_target_pairs={{0,16},{4,20},{8,24},{12,28},{16,0},{20,4},{24,8},{28,12},{1,17},{... | collective-permute-start | bytes 884744 | tf_op jit(solution)/shard_map/ppermute | solution.py:171
  129.5 18.4 %collective-permute-start.2 = (bf16[3,96,768]{2,1,0:T(8,128)(2,1)S(1)}, bf16[3,96,768]{2,1,0:T(8,128)(2,1)S(1)}, u32[]{:S(2)}, u32[]{:S(2)}) collective-permute-start(bf16[3,96,768]{2,1,0:T(8,128)(2,1)S(1)} %reshape.576), channel_id=1, source_target_pairs={{0,8},{4,12},{8,0},{12,4},{16,24},{20,28},{24,16},{28,20},{1,9},{5... | collective-permute-start | bytes 1327112 | tf_op jit(solution)/shard_map/ppermute | solution.py:171
  140.6 20.0 %collective-permute-start.22 = (bf16[96,3072]{1,0:T(8,128)(2,1)S(1)}, bf16[96,3072]{1,0:T(8,128)(2,1)S(1)}, u32[]{:S(2)}, u32[]{:S(2)}) collective-permute-start(bf16[96,3072]{1,0:T(8,128)(2,1)S(1)} %bitcast.806), channel_id=1, source_target_pairs={{0,16},{4,20},{8,24},{12,28},{16,0},{20,4},{24,8},{28,12},{1,17},{... | collective-permute-start | bytes 1769480 | tf_op jit(solution)/shard_map/ppermute | solution.py:171
  143.4 18.6 %collective-permute-start.17 = (bf16[96,3072]{1,0:T(8,128)(2,1)S(1)}, bf16[96,3072]{1,0:T(8,128)(2,1)S(1)}, u32[]{:S(2)}, u32[]{:S(2)}) collective-permute-start(bf16[96,3072]{1,0:T(8,128)(2,1)S(1)} %bitcast.808), channel_id=1, source_target_pairs={{0,8},{4,12},{8,0},{12,4},{16,24},{20,28},{24,16},{28,20},{1,9},{5... | collective-permute-start | bytes 1769480 | tf_op jit(solution)/shard_map/ppermute | solution.py:171
  146.9 26.3 %collective-permute-start.42 = (bf16[96,3072]{1,0:T(8,128)(2,1)S(1)}, bf16[96,3072]{1,0:T(8,128)(2,1)S(1)}, u32[]{:S(2)}, u32[]{:S(2)}) collective-permute-start(bf16[96,3072]{1,0:T(8,128)(2,1)S(1)} %bitcast.810), channel_id=1, source_target_pairs={{0,16},{4,20},{8,24},{12,28},{16,0},{20,4},{24,8},{28,12},{1,17},{... | collective-permute-start | bytes 1769480 | tf_op jit(solution)/shard_map/ppermute | solution.py:171
  148.0 26.9 %collective-permute-start.37 = (bf16[96,3072]{1,0:T(8,128)(2,1)S(1)}, bf16[96,3072]{1,0:T(8,128)(2,1)S(1)}, u32[]{:S(2)}, u32[]{:S(2)}) collective-permute-start(bf16[96,3072]{1,0:T(8,128)(2,1)S(1)} %bitcast.812), channel_id=1, source_target_pairs={{0,8},{4,12},{8,0},{12,4},{16,24},{20,28},{24,16},{28,20},{1,9},{5... | collective-permute-start | bytes 1769480 | tf_op jit(solution)/shard_map/ppermute | solution.py:171
  149.9 36.1 %collective-permute-start.14 = (bf16[2,2,96,768]{3,2,1,0:T(8,128)(2,1)}, bf16[2,2,96,768]{3,2,1,0:T(8,128)(2,1)}, u32[]{:S(2)}, u32[]{:S(2)}) collective-permute-start(bf16[2,2,96,768]{3,2,1,0:T(8,128)(2,1)} %pad_maximum_fusion.21), channel_id=1, source_target_pairs={{0,4},{4,0},{8,12},{12,8},{16,20},{20,16},{24,28},{28,24},{1,5},{5... | collective-permute-start | bytes 1769480 | tf_op jit(solution)/shard_map/ppermute | solution.py:171
  160.6 18.6 %collective-permute-start.34 = (bf16[2,2,96,768]{3,2,1,0:T(8,128)(2,1)S(1)}, bf16[2,2,96,768]{3,2,1,0:T(8,128)(2,1)S(1)}, u32[]{:S(2)}, u32[]{:S(2)}) collective-permute-start(bf16[2,2,96,768]{3,2,1,0:T(8,128)(2,1)S(1)} %pad_maximum_fusion.25), channel_id=1, source_target_pairs={{0,4},{4,0},{8,12},{12,8},{16,20},{20,16},{24,28},{28,24},{1,5},{5... | collective-permute-start | bytes 1769480 | tf_op jit(solution)/shard_map/ppermute | solution.py:171
  162.1 38.2 %collective-permute-start.3 = (bf16[3,2,96,768]{3,2,0,1:T(8,128)(2,1)}, bf16[3,2,96,768]{3,2,0,1:T(8,128)(2,1)}, u32[]{:S(2)}, u32[]{:S(2)}) collective-permute-start(bf16[3,2,96,768]{3,2,0,1:T(8,128)(2,1)} %pad_maximum_fusion.18), channel_id=1, source_target_pairs={{0,16},{4,20},{8,24},{12,28},{16,0},{20,4},{24,8},{28,12},{1,17},{... | collective-permute-start | bytes 2654216 | tf_op jit(solution)/shard_map/ppermute | solution.py:171
  173.2 29.9 %collective-permute-start.28 = (bf16[3,2,96,768]{3,2,0,1:T(8,128)(2,1)}, bf16[3,2,96,768]{3,2,0,1:T(8,128)(2,1)}, u32[]{:S(2)}, u32[]{:S(2)}) collective-permute-start(bf16[3,2,96,768]{3,2,0,1:T(8,128)(2,1)} %pad_maximum_fusion.19), channel_id=1, source_target_pairs={{0,8},{4,12},{8,0},{12,4},{16,24},{20,28},{24,16},{28,20},{1,9},{5... | collective-permute-start | bytes 2654216 | tf_op jit(solution)/shard_map/ppermute | solution.py:171
  174.8 46.6 %collective-permute-start.23 = (bf16[2,96,3072]{2,1,0:T(8,128)(2,1)}, bf16[2,96,3072]{2,1,0:T(8,128)(2,1)}, u32[]{:S(2)}, u32[]{:S(2)}) collective-permute-start(bf16[2,96,3072]{2,1,0:T(8,128)(2,1)} %pad_maximum_fusion.14), channel_id=1, source_target_pairs={{0,8},{4,12},{8,0},{12,4},{16,24},{20,28},{24,16},{28,20},{1,9},{5... | collective-permute-start | bytes 3538952 | tf_op jit(solution)/shard_map/ppermute | solution.py:171
  179.2 43.9 %collective-permute-start.18 = (bf16[2,96,3072]{2,1,0:T(8,128)(2,1)}, bf16[2,96,3072]{2,1,0:T(8,128)(2,1)}, u32[]{:S(2)}, u32[]{:S(2)}) collective-permute-start(bf16[2,96,3072]{2,1,0:T(8,128)(2,1)} %pad_maximum_fusion.13), channel_id=1, source_target_pairs={{0,16},{4,20},{8,24},{12,28},{16,0},{20,4},{24,8},{28,12},{1,17},{... | collective-permute-start | bytes 3538952 | tf_op jit(solution)/shard_map/ppermute | solution.py:171
  181.7 17.3 %all-to-all-start.2 = ((bf16[4,128,768]{2,1,0:T(8,128)(2,1)}), bf16[4,128,768]{2,1,0:T(8,128)(2,1)S(1)}, u32[]{:S(2)}, u32[]{:S(2)}) async-start(bf16[4,128,768]{2,1,0:T(8,128)(2,1)} %pad.8), calls=%async_computation.2 | async-start | bytes 1572864 | tf_op jit(solution)/shard_map/all_to_all | solution.py:141
  185.9 53.6 %collective-permute-start.43 = (bf16[2,96,3072]{2,1,0:T(8,128)(2,1)}, bf16[2,96,3072]{2,1,0:T(8,128)(2,1)}, u32[]{:S(2)}, u32[]{:S(2)}) collective-permute-start(bf16[2,96,3072]{2,1,0:T(8,128)(2,1)} %pad_maximum_fusion.17), channel_id=1, source_target_pairs={{0,8},{4,12},{8,0},{12,4},{16,24},{20,28},{24,16},{28,20},{1,9},{5... | collective-permute-start | bytes 3538952 | tf_op jit(solution)/shard_map/ppermute | solution.py:171
  200.3 42.4 %collective-permute-start.38 = (bf16[2,96,3072]{2,1,0:T(8,128)(2,1)}, bf16[2,96,3072]{2,1,0:T(8,128)(2,1)S(1)}, u32[]{:S(2)}, u32[]{:S(2)}) collective-permute-start(bf16[2,96,3072]{2,1,0:T(8,128)(2,1)} %pad_maximum_fusion.16), channel_id=1, source_target_pairs={{0,16},{4,20},{8,24},{12,28},{16,0},{20,4},{24,8},{28,12},{1,17},{... | collective-permute-start | bytes 3538952 | tf_op jit(solution)/shard_map/ppermute | solution.py:171
  203.1 41.9 %collective-permute-start.4 = (bf16[3,2,2,96,768]{4,3,0,2,1:T(8,128)(2,1)S(1)}, bf16[3,2,2,96,768]{4,3,0,2,1:T(8,128)(2,1)S(1)}, u32[]{:S(2)}, u32[]{:S(2)}) collective-permute-start(bf16[3,2,2,96,768]{4,3,0,2,1:T(8,128)(2,1)S(1)} %pad_maximum_fusion.10), channel_id=1, source_target_pairs={{0,4},{4,0},{8,12},{12,8},{16,20},{20,16},{24,28},{28,24},{1,5},{5... | collective-permute-start | bytes 5308424 | tf_op jit(solution)/shard_map/ppermute | solution.py:171
  221.4 24.5 %collective-permute-start.29 = (bf16[3,2,2,96,768]{4,3,0,2,1:T(8,128)(2,1)}, bf16[3,2,2,96,768]{4,3,0,2,1:T(8,128)(2,1)S(1)}, u32[]{:S(2)}, u32[]{:S(2)}) collective-permute-start(bf16[3,2,2,96,768]{4,3,0,2,1:T(8,128)(2,1)} %pad_maximum_fusion.11), channel_id=1, source_target_pairs={{0,4},{4,0},{8,12},{12,8},{16,20},{20,16},{24,28},{28,24},{1,5},{5... | collective-permute-start | bytes 5308424 | tf_op jit(solution)/shard_map/ppermute | solution.py:171
  223.1 42.5 %collective-permute-start.24 = (bf16[2,2,96,3072]{3,2,0,1:T(8,128)(2,1)S(1)}, bf16[2,2,96,3072]{3,2,0,1:T(8,128)(2,1)}, u32[]{:S(2)}, u32[]{:S(2)}) collective-permute-start(bf16[2,2,96,3072]{3,2,0,1:T(8,128)(2,1)S(1)} %pad_maximum_fusion.7), channel_id=1, source_target_pairs={{0,4},{4,0},{8,12},{12,8},{16,20},{20,16},{24,28},{28,24},{1,5},{5... | collective-permute-start | bytes 7077896 | tf_op jit(solution)/shard_map/ppermute | solution.py:171
  239.6 31.4 %collective-permute-start.19 = (bf16[2,2,96,3072]{3,2,1,0:T(8,128)(2,1)S(1)}, bf16[2,2,96,3072]{3,2,1,0:T(8,128)(2,1)}, u32[]{:S(2)}, u32[]{:S(2)}) collective-permute-start(bf16[2,2,96,3072]{3,2,1,0:T(8,128)(2,1)S(1)} %pad_maximum_fusion.6), channel_id=1, source_target_pairs={{0,4},{4,0},{8,12},{12,8},{16,20},{20,16},{24,28},{28,24},{1,5},{5... | collective-permute-start | bytes 7077896 | tf_op jit(solution)/shard_map/ppermute | solution.py:171
  242.7 33.4 %collective-permute-start.44 = (bf16[2,2,96,3072]{3,2,1,0:T(8,128)(2,1)}, bf16[2,2,96,3072]{3,2,1,0:T(8,128)(2,1)}, u32[]{:S(2)}, u32[]{:S(2)}) collective-permute-start(bf16[2,2,96,3072]{3,2,1,0:T(8,128)(2,1)} %pad_maximum_fusion.9), channel_id=1, source_target_pairs={{0,4},{4,0},{8,12},{12,8},{16,20},{20,16},{24,28},{28,24},{1,5},{5... | collective-permute-start | bytes 7077896 | tf_op jit(solution)/shard_map/ppermute | solution.py:171
  245.0 65.2 %collective-permute-start.39 = (bf16[2,2,96,3072]{3,2,1,0:T(8,128)(2,1)}, bf16[2,2,96,3072]{3,2,1,0:T(8,128)(2,1)}, u32[]{:S(2)}, u32[]{:S(2)}) collective-permute-start(bf16[2,2,96,3072]{3,2,1,0:T(8,128)(2,1)} %pad_maximum_fusion.8), channel_id=1, source_target_pairs={{0,4},{4,0},{8,12},{12,8},{16,20},{20,16},{24,28},{28,24},{1,5},{5... | collective-permute-start | bytes 7077896 | tf_op jit(solution)/shard_map/ppermute | solution.py:171
  404.5 106.8 %all-to-all-start.1 = ((bf16[4,128,768]{2,1,0:T(8,128)(2,1)}), bf16[4,128,768]{2,1,0:T(8,128)(2,1)}, u32[]{:S(2)}, u32[]{:S(2)}) async-start(bf16[4,128,768]{2,1,0:T(8,128)(2,1)} %bitcast.846), calls=%async_computation.1 | async-start | bytes 1572864 | tf_op jit(solution)/shard_map/all_to_all | solution.py:148
  439.5 96.3 %collective-permute-start.55 = (bf16[3,2,2,96,768]{4,3,2,1,0:T(8,128)(2,1)}, bf16[3,2,2,96,768]{4,3,2,1,0:T(8,128)(2,1)}, u32[]{:S(2)}, u32[]{:S(2)}) collective-permute-start(bf16[3,2,2,96,768]{4,3,2,1,0:T(8,128)(2,1)} %dynamic-slice_bitcast_fusion.4), channel_id=1, source_target_pairs={{0,4},{4,0},{8,12},{12,8},{16,20},{20,16},{24,28},{28,24},{1,5},{5... | collective-permute-start | bytes 5308424 | tf_op jit(solution)/shard_map/ppermute | solution.py:181
  442.7 30.9 %collective-permute-start.65 = (bf16[2,2,96,768]{3,2,1,0:T(8,128)(2,1)}, bf16[2,2,96,768]{3,2,1,0:T(8,128)(2,1)}, u32[]{:S(2)}, u32[]{:S(2)}) collective-permute-start(bf16[2,2,96,768]{3,2,1,0:T(8,128)(2,1)} %dynamic-slice_bitcast_fusion.16), channel_id=1, source_target_pairs={{0,4},{4,0},{8,12},{12,8},{16,20},{20,16},{24,28},{28,24},{1,5},{5... | collective-permute-start | bytes 1769480 | tf_op jit(solution)/shard_map/ppermute | solution.py:181
  450.3 88.8 %collective-permute-start.50 = (bf16[3,2,2,96,768]{4,3,2,1,0:T(8,128)(2,1)}, bf16[3,2,2,96,768]{4,3,2,1,0:T(8,128)(2,1)}, u32[]{:S(2)}, u32[]{:S(2)}) collective-permute-start(bf16[3,2,2,96,768]{4,3,2,1,0:T(8,128)(2,1)} %dynamic-slice_bitcast_fusion.5), channel_id=1, source_target_pairs={{0,4},{4,0},{8,12},{12,8},{16,20},{20,16},{24,28},{28,24},{1,5},{5... | collective-permute-start | bytes 5308424 | tf_op jit(solution)/shard_map/ppermute | solution.py:181
  453.0 22.3 %collective-permute-start.60 = (bf16[2,2,96,768]{3,2,1,0:T(8,128)(2,1)}, bf16[2,2,96,768]{3,2,1,0:T(8,128)(2,1)}, u32[]{:S(2)}, u32[]{:S(2)}) collective-permute-start(bf16[2,2,96,768]{3,2,1,0:T(8,128)(2,1)} %dynamic-slice_bitcast_fusion.17), channel_id=1, source_target_pairs={{0,4},{4,0},{8,12},{12,8},{16,20},{20,16},{24,28},{28,24},{1,5},{5... | collective-permute-start | bytes 1769480 | tf_op jit(solution)/shard_map/ppermute | solution.py:181
  469.4 73.5 %collective-permute-start.75 = (bf16[2,2,96,3072]{3,2,1,0:T(8,128)(2,1)}, bf16[2,2,96,3072]{3,2,1,0:T(8,128)(2,1)}, u32[]{:S(2)}, u32[]{:S(2)}) collective-permute-start(bf16[2,2,96,3072]{3,2,1,0:T(8,128)(2,1)} %dynamic-slice_bitcast_fusion.2), channel_id=1, source_target_pairs={{0,4},{4,0},{8,12},{12,8},{16,20},{20,16},{24,28},{28,24},{1,5},{5... | collective-permute-start | bytes 7077896 | tf_op jit(solution)/shard_map/ppermute | solution.py:181
  473.6 73.8 %collective-permute-start.70 = (bf16[2,2,96,3072]{3,2,1,0:T(8,128)(2,1)}, bf16[2,2,96,3072]{3,2,1,0:T(8,128)(2,1)}, u32[]{:S(2)}, u32[]{:S(2)}) collective-permute-start(bf16[2,2,96,3072]{3,2,1,0:T(8,128)(2,1)} %dynamic-slice_bitcast_fusion.3), channel_id=1, source_target_pairs={{0,4},{4,0},{8,12},{12,8},{16,20},{20,16},{24,28},{28,24},{1,5},{5... | collective-permute-start | bytes 7077896 | tf_op jit(solution)/shard_map/ppermute | solution.py:181
  511.3 23.4 %all-to-all-start.3 = ((bf16[4,128,768]{2,1,0:T(8,128)(2,1)}), bf16[4,128,768]{2,1,0:T(8,128)(2,1)S(1)}, u32[]{:S(2)}, u32[]{:S(2)}) async-start(bf16[4,128,768]{2,1,0:T(8,128)(2,1)} %bitcast.165), calls=%async_computation.3 | async-start | bytes 1572864 | tf_op jit(solution)/shard_map/all_to_all | solution.py:148
  532.0 20.8 %collective-permute-start.85 = (bf16[2,2,96,3072]{3,2,1,0:T(8,128)(2,1)}, bf16[2,2,96,3072]{3,2,1,0:T(8,128)(2,1)}, u32[]{:S(2)}, u32[]{:S(2)}) collective-permute-start(bf16[2,2,96,3072]{3,2,1,0:T(8,128)(2,1)} %dynamic-slice_bitcast_fusion), channel_id=1, source_target_pairs={{0,4},{4,0},{8,12},{12,8},{16,20},{20,16},{24,28},{28,24},{1,5},{5... | collective-permute-start | bytes 7077896 | tf_op jit(solution)/shard_map/ppermute | solution.py:181
  535.8 22.2 %collective-permute-start.80 = (bf16[2,2,96,3072]{3,2,1,0:T(8,128)(2,1)}, bf16[2,2,96,3072]{3,2,1,0:T(8,128)(2,1)S(1)}, u32[]{:S(2)}, u32[]{:S(2)}) collective-permute-start(bf16[2,2,96,3072]{3,2,1,0:T(8,128)(2,1)} %dynamic-slice_bitcast_fusion.1), channel_id=1, source_target_pairs={{0,4},{4,0},{8,12},{12,8},{16,20},{20,16},{24,28},{28,24},{1,5},{5... | collective-permute-start | bytes 7077896 | tf_op jit(solution)/shard_map/ppermute | solution.py:181
  539.0 22.0 %collective-permute-start.56 = (bf16[3,2,96,768]{3,2,1,0:T(8,128)(2,1)S(1)}, bf16[3,2,96,768]{3,2,1,0:T(8,128)(2,1)S(1)}, u32[]{:S(2)}, u32[]{:S(2)}) collective-permute-start(bf16[3,2,96,768]{3,2,1,0:T(8,128)(2,1)S(1)} %dynamic-slice_bitcast_fusion.10), channel_id=1, source_target_pairs={{0,8},{4,12},{8,0},{12,4},{16,24},{20,28},{24,16},{28,20},{1,9},{5... | collective-permute-start | bytes 2654216 | tf_op jit(solution)/shard_map/ppermute | solution.py:181
  542.9 22.6 %collective-permute-start.51 = (bf16[3,2,96,768]{3,2,1,0:T(8,128)(2,1)S(1)}, bf16[3,2,96,768]{3,2,1,0:T(8,128)(2,1)S(1)}, u32[]{:S(2)}, u32[]{:S(2)}) collective-permute-start(bf16[3,2,96,768]{3,2,1,0:T(8,128)(2,1)S(1)} %dynamic-slice_bitcast_fusion.11), channel_id=1, source_target_pairs={{0,16},{4,20},{8,24},{12,28},{16,0},{20,4},{24,8},{28,12},{1,17},{... | collective-permute-start | bytes 2654216 | tf_op jit(solution)/shard_map/ppermute | solution.py:181
  547.4 124.7 %collective-permute-start.76 = (bf16[2,96,3072]{2,1,0:T(8,128)(2,1)}, bf16[2,96,3072]{2,1,0:T(8,128)(2,1)}, u32[]{:S(2)}, u32[]{:S(2)}) collective-permute-start(bf16[2,96,3072]{2,1,0:T(8,128)(2,1)} %dynamic-slice_bitcast_fusion.8), channel_id=1, source_target_pairs={{0,16},{4,20},{8,24},{12,28},{16,0},{20,4},{24,8},{28,12},{1,17},{... | collective-permute-start | bytes 3538952 | tf_op jit(solution)/shard_map/ppermute | solution.py:181
  552.8 122.8 %collective-permute-start.71 = (bf16[2,96,3072]{2,1,0:T(8,128)(2,1)}, bf16[2,96,3072]{2,1,0:T(8,128)(2,1)}, u32[]{:S(2)}, u32[]{:S(2)}) collective-permute-start(bf16[2,96,3072]{2,1,0:T(8,128)(2,1)} %dynamic-slice_bitcast_fusion.9), channel_id=1, source_target_pairs={{0,16},{4,20},{8,24},{12,28},{16,0},{20,4},{24,8},{28,12},{1,17},{... | collective-permute-start | bytes 3538952 | tf_op jit(solution)/shard_map/ppermute | solution.py:181
  558.0 119.9 %collective-permute-start.86 = (bf16[2,96,3072]{2,1,0:T(8,128)(2,1)}, bf16[2,96,3072]{2,1,0:T(8,128)(2,1)}, u32[]{:S(2)}, u32[]{:S(2)}) collective-permute-start(bf16[2,96,3072]{2,1,0:T(8,128)(2,1)} %dynamic-slice_bitcast_fusion.6), channel_id=1, source_target_pairs={{0,8},{4,12},{8,0},{12,4},{16,24},{20,28},{24,16},{28,20},{1,9},{5... | collective-permute-start | bytes 3538952 | tf_op jit(solution)/shard_map/ppermute | solution.py:181
  561.3 63.0 %collective-permute-start.57 = (bf16[3,96,768]{2,1,0:T(8,128)(2,1)S(1)}, bf16[3,96,768]{2,1,0:T(8,128)(2,1)S(1)}, u32[]{:S(2)}, u32[]{:S(2)}) collective-permute-start(bf16[3,96,768]{2,1,0:T(8,128)(2,1)S(1)} %dynamic-slice_bitcast_fusion.18), channel_id=1, source_target_pairs={{0,16},{4,20},{8,24},{12,28},{16,0},{20,4},{24,8},{28,12},{1,17},{... | collective-permute-start | bytes 1327112 | tf_op jit(solution)/shard_map/ppermute | solution.py:181
  566.5 64.3 %collective-permute-start.52 = (bf16[3,96,768]{2,1,0:T(8,128)(2,1)}, bf16[3,96,768]{2,1,0:T(8,128)(2,1)}, u32[]{:S(2)}, u32[]{:S(2)}) collective-permute-start(bf16[3,96,768]{2,1,0:T(8,128)(2,1)} %dynamic-slice_bitcast_fusion.19), channel_id=1, source_target_pairs={{0,8},{4,12},{8,0},{12,4},{16,24},{20,28},{24,16},{28,20},{1,9},{5... | collective-permute-start | bytes 1327112 | tf_op jit(solution)/shard_map/ppermute | solution.py:181
  624.2 56.4 %collective-permute-start.81 = (bf16[2,96,3072]{2,1,0:T(8,128)(2,1)}, bf16[2,96,3072]{2,1,0:T(8,128)(2,1)}, u32[]{:S(2)}, u32[]{:S(2)}) collective-permute-start(bf16[2,96,3072]{2,1,0:T(8,128)(2,1)} %dynamic-slice_bitcast_fusion.7), channel_id=1, source_target_pairs={{0,8},{4,12},{8,0},{12,4},{16,24},{20,28},{24,16},{28,20},{1,9},{5... | collective-permute-start | bytes 3538952 | tf_op jit(solution)/shard_map/ppermute | solution.py:181
  674.0 16.3 %collective-permute-start.77 = (bf16[96,3072]{1,0:T(8,128)(2,1)S(1)}, bf16[96,3072]{1,0:T(8,128)(2,1)S(1)}, u32[]{:S(2)}, u32[]{:S(2)}) collective-permute-start(bf16[96,3072]{1,0:T(8,128)(2,1)S(1)} %dynamic-slice_bitcast_fusion.14), channel_id=1, source_target_pairs={{0,8},{4,12},{8,0},{12,4},{16,24},{20,28},{24,16},{28,20},{1,9},{5... | collective-permute-start | bytes 1769480 | tf_op jit(solution)/shard_map/ppermute | solution.py:181
  677.3 22.6 %collective-permute-start.72 = (bf16[96,3072]{1,0:T(8,128)(2,1)S(1)}, bf16[96,3072]{1,0:T(8,128)(2,1)S(1)}, u32[]{:S(2)}, u32[]{:S(2)}) collective-permute-start(bf16[96,3072]{1,0:T(8,128)(2,1)S(1)} %dynamic-slice_bitcast_fusion.15), channel_id=1, source_target_pairs={{0,8},{4,12},{8,0},{12,4},{16,24},{20,28},{24,16},{28,20},{1,9},{5... | collective-permute-start | bytes 1769480 | tf_op jit(solution)/shard_map/ppermute | solution.py:181
  679.8 21.8 %collective-permute-start.87 = (bf16[96,3072]{1,0:T(8,128)(2,1)S(1)}, bf16[96,3072]{1,0:T(8,128)(2,1)S(1)}, u32[]{:S(2)}, u32[]{:S(2)}) collective-permute-start(bf16[96,3072]{1,0:T(8,128)(2,1)S(1)} %dynamic-slice_bitcast_fusion.12), channel_id=1, source_target_pairs={{0,16},{4,20},{8,24},{12,28},{16,0},{20,4},{24,8},{28,12},{1,17},{... | collective-permute-start | bytes 1769480 | tf_op jit(solution)/shard_map/ppermute | solution.py:181
  682.4 22.8 %collective-permute-start.82 = (bf16[96,3072]{1,0:T(8,128)(2,1)S(1)}, bf16[96,3072]{1,0:T(8,128)(2,1)S(1)}, u32[]{:S(2)}, u32[]{:S(2)}) collective-permute-start(bf16[96,3072]{1,0:T(8,128)(2,1)S(1)} %dynamic-slice_bitcast_fusion.13), channel_id=1, source_target_pairs={{0,16},{4,20},{8,24},{12,28},{16,0},{20,4},{24,8},{28,12},{1,17},{... | collective-permute-start | bytes 1769480 | tf_op jit(solution)/shard_map/ppermute | solution.py:181
  690.5 16.3 %collective-permute-start.78 = (bf16[2,96,768]{2,1,0:T(8,128)(2,1)S(1)}, bf16[2,96,768]{2,1,0:T(8,128)(2,1)S(1)}, u32[]{:S(2)}, u32[]{:S(2)}) collective-permute-start(bf16[2,96,768]{2,1,0:T(8,128)(2,1)S(1)} %dynamic-slice_bitcast_fusion.22), channel_id=1, source_target_pairs={{0,2},{1,3},{2,0},{3,1},{4,6},{5,7},{6,4},{7,5},{8,10},{9,11},{10,... | collective-permute-start | bytes 884744 | tf_op jit(solution)/shard_map/ppermute | solution.py:181
  700.2 27.0 %collective-permute-start.73 = (bf16[2,96,768]{2,1,0:T(8,128)(2,1)S(1)}, bf16[2,96,768]{2,1,0:T(8,128)(2,1)S(1)}, u32[]{:S(2)}, u32[]{:S(2)}) collective-permute-start(bf16[2,96,768]{2,1,0:T(8,128)(2,1)S(1)} %dynamic-slice_bitcast_fusion.23), channel_id=1, source_target_pairs={{0,2},{1,3},{2,0},{3,1},{4,6},{5,7},{6,4},{7,5},{8,10},{9,11},{10,... | collective-permute-start | bytes 884744 | tf_op jit(solution)/shard_map/ppermute | solution.py:181
  701.8 31.8 %collective-permute-start.88 = (bf16[2,96,768]{2,1,0:T(8,128)(2,1)S(1)}, bf16[2,96,768]{2,1,0:T(8,128)(2,1)S(1)}, u32[]{:S(2)}, u32[]{:S(2)}) collective-permute-start(bf16[2,96,768]{2,1,0:T(8,128)(2,1)S(1)} %dynamic-slice_bitcast_fusion.20), channel_id=1, source_target_pairs={{0,2},{1,3},{2,0},{3,1},{4,6},{5,7},{6,4},{7,5},{8,10},{9,11},{10,... | collective-permute-start | bytes 884744 | tf_op jit(solution)/shard_map/ppermute | solution.py:181
  705.4 33.8 %collective-permute-start.83 = (bf16[2,96,768]{2,1,0:T(8,128)(2,1)S(1)}, bf16[2,96,768]{2,1,0:T(8,128)(2,1)S(1)}, u32[]{:S(2)}, u32[]{:S(2)}) collective-permute-start(bf16[2,96,768]{2,1,0:T(8,128)(2,1)S(1)} %dynamic-slice_bitcast_fusion.21), channel_id=1, source_target_pairs={{0,2},{1,3},{2,0},{3,1},{4,6},{5,7},{6,4},{7,5},{8,10},{9,11},{10,... | collective-permute-start | bytes 884744 | tf_op jit(solution)/shard_map/ppermute | solution.py:181
  706.9 32.5 %collective-permute-start.79 = (bf16[96,768]{1,0:T(8,128)(2,1)S(1)}, bf16[96,768]{1,0:T(8,128)(2,1)S(1)}, u32[]{:S(2)}, u32[]{:S(2)}) collective-permute-start(bf16[96,768]{1,0:T(8,128)(2,1)S(1)} %dynamic-slice_bitcast_fusion.30), channel_id=1, source_target_pairs={{0,1},{1,0},{2,3},{3,2},{4,5},{5,4},{6,7},{7,6},{8,9},{9,8},{10,11... | collective-permute-start | bytes 442376 | tf_op jit(solution)/shard_map/ppermute | solution.py:181
  (146 other events, 1628.8 us)
